TPU v7x, 512 devices: a whole 4x4x16 slice. The times are simulated.
512 devices in a mesh: expert: 8 (over z_hi, y), blk: 64 (over x, z_lo, core).
Axes of the slice: x: 4, y: 4, z: 16 (z_hi: 2, z_lo: 8; z = z_hi * 8 + z_lo), core: 2. Of those that a mesh axis runs over, the one named last changes fastest.
Arguments:
- tokens: bfloat16 [2048, 6144], P('expert', 'blk'), may hold values from -6 to 6
- expert_ids: int32 [2048, 2], P('expert'), may hold values from 0 to 7, all different within a row
- routing_weights: float32 [2048, 2], P('expert'), may hold values from 0.2 to 1
- gate_weight: bfloat16 [8, 6144, 8192], P('expert', None, 'blk'), may hold values from -0.078125 to 0.078125
- up_weight: bfloat16 [8, 6144, 8192], P('expert', None, 'blk'), may hold values from -0.078125 to 0.078125
- down_weight: bfloat16 [8, 8192, 6144], P('expert', None, 'blk'), may hold values from -0.0625 to 0.0625
Outputs:
- mixed: bfloat16 [2048, 6144], P('expert', 'blk')
Inputs may be any that keep to these rules, and one draw needn't show every extreme that they name: `expert_ids`: each row names two different experts.
All inputs are finite; a program needn't handle non-finite values.
Results may differ from a plain program's by a relative error of at most 0.0057.
Values may be sent and summed in bfloat16 or wider, within the bound.
No kernel may reach another device: no remote copies, remote signals or barrier semaphores. Data moves between devices by JAX's collectives and lax.ppermute only.
A program may use at most 64 MiB of HBM per device.

v0:
```python
import jax
import jax.numpy as jnp
from jax import lax
from jax.sharding import PartitionSpec as P


def route_shard(ids, experts, capacity):
    flat = ids.reshape(-1)
    onehot = (flat[:, None] == jnp.arange(experts, dtype=jnp.int32)[None, :]).astype(jnp.int32)
    earlier = jnp.cumsum(onehot, axis=0) - onehot
    slot = jnp.sum(earlier * onehot, axis=1).reshape(ids.shape)
    kept = slot < capacity
    target = jnp.where(kept, ids * capacity + slot, -1)
    return (target, kept)


def local(tokens, expert_ids, routing_weights, gate_weight, up_weight, down_weight):
    experts = lax.axis_size("expert")
    tok_rows = tokens.shape[0]
    capacity = tok_rows * 2 // experts
    slots_all = experts * capacity
    target, kept = route_shard(expert_ids, experts, capacity)
    slot_index = lax.iota(jnp.int32, slots_all)
    first_hit = target[:, 0][None, :] == slot_index[:, None]
    second_hit = target[:, 1][None, :] == slot_index[:, None]
    select = (first_hit | second_hit).astype(jnp.bfloat16)
    w_gate = gate_weight[0]
    w_up = up_weight[0]
    w_down = down_weight[0]
    packed = jnp.dot(select, tokens, preferred_element_type=jnp.float32).astype(jnp.bfloat16)
    packed = packed.reshape(experts, capacity, tokens.shape[1])
    arrived = lax.all_to_all(packed, "expert", split_axis=0, concat_axis=0, tiled=True)
    arrived = arrived.reshape(slots_all, tokens.shape[1])
    piece = lax.all_gather(arrived, "blk", axis=1, tiled=True)
    gate_sum = jnp.dot(piece, w_gate, preferred_element_type=jnp.float32)
    up_sum = jnp.dot(piece, w_up, preferred_element_type=jnp.float32)
    hidden = (jax.nn.silu(gate_sum) * up_sum).astype(jnp.bfloat16)
    expert_out = jnp.dot(
        lax.all_gather(hidden, "blk", axis=1, tiled=True),
        w_down,
        preferred_element_type=jnp.float32,
    ).astype(jnp.bfloat16)
    returned = lax.all_to_all(
        expert_out.reshape(experts, capacity, w_down.shape[1]),
        "expert",
        split_axis=0,
        concat_axis=0,
        tiled=True,
    )
    returned = returned.reshape(slots_all, w_down.shape[1]).astype(jnp.float32)
    weight_first = jnp.where(kept[:, 0], routing_weights[:, 0], jnp.float32(0.0))
    weight_second = jnp.where(kept[:, 1], routing_weights[:, 1], jnp.float32(0.0))
    mixing = jnp.where(first_hit.T, weight_first[:, None], jnp.float32(0.0))
    mixing = mixing + jnp.where(second_hit.T, weight_second[:, None], jnp.float32(0.0))
    mixed = jnp.dot(
        mixing, returned, precision=lax.Precision.HIGHEST, preferred_element_type=jnp.float32
    )
    return mixed.astype(jnp.bfloat16)


def solution(mesh):
    placed = (
        P("expert", "blk"),
        P("expert", None),
        P("expert", None),
        P("expert", None, "blk"),
        P("expert", None, "blk"),
        P("expert", None, "blk"),
    )
    return jax.shard_map(
        local, mesh=mesh, in_specs=placed, out_specs=P("expert", "blk"), check_vma=False
    )
```

profile of v0, /device:TPU:38, one launch (start us, length us, event | category | flops | bytes accessed | tf_op | source)
XLA Modules:
  0.0 352.1 jit_solution(16333675620039946460)
XLA Ops:
  6.5 0.8 broadcast_multiply_fusion
  7.3 0.8 copy.23
  8.2 0.1 eq.73
  8.3 0.1 eq.69
  8.4 0.1 copy.26
  8.6 1.1 reduce-window.6
  9.8 0.2 slice_reduce_fusion.2
  10.0 0.1 fusion.28
  10.1 0.1 reshape.35
  10.3 0.2 slice_reduce_fusion.1
  10.5 1.1 convolution_convert_fusion
  11.5 0.1 copy.29
  11.7 35.6 %all_to_all.10 = bf16[8,64,96]{2,1,0:T(8,128)(2,1)S(1)} all-to-all(bf16[8,64,96]{2,1,0:T(8,128)(2,1)S(1)} %bitcast.32), channel_id=1, replica_groups=mesh['expert'=8,'blk'=64] {'expert'}, dimensions={0} | all-to-all | bytes 196608 | tf_op jit(solution)/shard_map/all_to_all | solution.py:32
  47.3 0.7 copy.30
  48.0 0.0 all-gather.3.cloned.1.call-update
  48.0 0.0 all-gather.5.cloned.1.call-start
  48.1 113.4 %all-gather.3.cloned.1.call-done = bf16[512,6144]{0,1:T(8,128)(2,1)} async-done(((bf16[512,96]{0,1:T(8,128)(2,1)}), bf16[512,6144]{0,1:T(8,128)(2,1)}) %all-gather.3.cloned.1.call-update) | async-done | bytes 6291472 | tf_op jit(solution)/shard_map/all_gather | solution.py:34
  161.5 4.8 %fusion.4 = f32[512,128]{1,0:T(8,128)S(1)} fusion(bf16[512,6144]{0,1:T(8,128)(2,1)} %all-gather.3.cloned.1.call-done, bf16[1,6144,128]{2,1,0:T(8,128)(2,1)S(1)} %copy-done), kind=kOutput, calls=%fused_computation.4 | convolution fusion | flops 805306368 | bytes 8126464 | tf_op jit(solution)/shard_map/dot_general | solution.py:35
  166.3 0.0 copy-start.2
  166.3 0.0 copy-start.1
  166.3 4.0 %fusion.9 = bf16[512,128]{1,0:T(8,128)(2,1)} fusion(bf16[512,6144]{0,1:T(8,128)(2,1)S(1)} %copy-done.3, bf16[1,6144,128]{2,1,0:T(8,128)(2,1)} %param.10, f32[512,128]{1,0:T(8,128)S(1)} %fusion.4), kind=kOutput, calls=%fused_computation.7 | convolution fusion | flops 805699584 | bytes 8257536 | tf_op jit(solution)/shard_map/dot_general | solution.py:36
  170.3 0.0 all-gather.5.cloned.1.call-update
  170.4 0.1 copy.28
  170.5 0.1 copy.27
  170.7 135.6 %all-gather.5.cloned.1.call-done = bf16[512,8192]{1,0:T(8,128)(2,1)} async-done(((bf16[512,128]{1,0:T(8,128)(2,1)}), bf16[512,8192]{1,0:T(8,128)(2,1)}) %all-gather.5.cloned.1.call-update) | async-done | bytes 8388624 | tf_op jit(solution)/shard_map/all_gather | solution.py:39
  306.2 0.0 copy-done.1
  306.2 6.8 %fusion.12 = bf16[512,96]{0,1:T(8,128)(2,1)} fusion(bf16[512,8192]{1,0:T(8,128)(2,1)} %all-gather.5.cloned.1.call-done, bf16[1,8192,96]{1,2,0:T(8,128)(2,1)S(1)} %copy-done.1), kind=kOutput, calls=%fused_computation.8 | convolution fusion | flops 805355520 | bytes 10059776 | tf_op jit(solution)/shard_map/dot_general | solution.py:38
  313.0 1.6 copy.31
  314.7 10.0 %all-to-all-start.1 = ((bf16[8,64,96]{2,1,0:T(8,128)(2,1)}), bf16[8,64,96]{2,1,0:T(8,128)(2,1)S(1)}, u32[]{:S(2)}, u32[]{:S(2)}) async-start(bf16[8,64,96]{2,1,0:T(8,128)(2,1)} %bitcast.7), calls=%async_computation.1 | async-start | bytes 262144 | tf_op jit(solution)/shard_map/all_to_all | solution.py:43
  324.6 0.2 select_reduce_fusion.1
  324.8 19.2 %all-to-all-done.1 = bf16[8,64,96]{2,1,0:T(8,128)(2,1)S(1)} async-done(((bf16[8,64,96]{2,1,0:T(8,128)(2,1)}), bf16[8,64,96]{2,1,0:T(8,128)(2,1)S(1)}, u32[]{:S(2)}, u32[]{:S(2)}) %all-to-all-start.1) | async-done | bytes 98336 | tf_op jit(solution)/shard_map/all_to_all | solution.py:43
  344.1 1.2 convolution_convert_fusion.1
  (12 shorter events, 0.1 us)
Async XLA Ops:
  6.5 155.0 %copy-start = (bf16[1,6144,128]{2,1,0:T(8,128)(2,1)S(1)}, bf16[1,6144,128]{2,1,0:T(8,128)(2,1)}, u32[]{:S(2)}) copy-start(bf16[1,6144,128]{2,1,0:T(8,128)(2,1)} %param.9) | copy-start | bytes 4718596
  6.5 155.0 %all-gather.3.cloned.1.call-start = ((), (), s32[]{:S(2)}) async-start(), calls=%async_computation.2 | async-start | bytes 6389760 | tf_op jit(solution)/shard_map/all_gather | solution.py:34
  48.0 258.2 %all-gather.5.cloned.1.call-start = ((), (), s32[]{:S(2)}) async-start(), calls=%async_computation.3 | async-start | bytes 8519680 | tf_op jit(solution)/shard_map/all_gather | solution.py:39
  161.5 4.8 %copy-start.3 = (bf16[512,6144]{0,1:T(8,128)(2,1)S(1)}, bf16[512,6144]{0,1:T(8,128)(2,1)}, u32[]{:S(2)}) copy-start(bf16[512,6144]{0,1:T(8,128)(2,1)} %all-gather.3.cloned.1.call-done) | copy-start | bytes 18874372
  166.3 4.1 %copy-start.2 = (f32[256,2]{0,1:T(2,128)S(1)}, f32[256,2]{0,1:T(2,128)}, u32[]{:S(2)}) copy-start(f32[256,2]{0,1:T(2,128)} %param.8) | copy-start | bytes 6148
  166.3 139.9 %copy-start.1 = (bf16[1,8192,96]{1,2,0:T(8,128)(2,1)S(1)}, bf16[1,8192,96]{1,2,0:T(8,128)(2,1)}, u32[]{:S(2)}) copy-start(bf16[1,8192,96]{1,2,0:T(8,128)(2,1)} %param.11) | copy-start | bytes 4718596
  314.7 29.4 %all-to-all-start.1 = ((bf16[8,64,96]{2,1,0:T(8,128)(2,1)}), bf16[8,64,96]{2,1,0:T(8,128)(2,1)S(1)}, u32[]{:S(2)}, u32[]{:S(2)}) async-start(bf16[8,64,96]{2,1,0:T(8,128)(2,1)} %bitcast.7), calls=%async_computation.1 | async-start | bytes 262144 | tf_op jit(solution)/shard_map/all_to_all | solution.py:43
Sparse Core Ops, SparseCore 0:
  48.1 113.3 all-gather.2
  170.5 135.7 all-gather.4
where the time goes:
time: 352 us
  waiting for transfers between devices  268 us (76%)
  blocking collectives  35.6 us (10%)
  matrix products  17.8 us (5%)
  between operations  13.5 us (4%)
  starting transfers between devices  10 us (3%)
  local copies, waits for them, and re-layouts  4.57 us (1%)
    all_gather x1, waiting for transfers between devices, local(): lax.all_gather(hidden, 'blk', axis=1, tiled=True)  136 us
    all_gather x1, waiting for transfers between devices, local(): piece = lax.all_gather(arrived, 'blk', axis=1, tiled=True)  113 us
    all_to_all x1, blocking collectives, local(): lax.all_to_all(packed, 'expert', split_axis=0, concat_axis=0, tiled=True)  35.6 us
    all_to_all x1, waiting for transfers between devices, local(): lax.all_to_all(expert_out.reshape(experts, capacity, w_down.shape[1]), 'e...  19.2 us
    all_to_all x1, starting transfers between devices, local(): lax.all_to_all(expert_out.reshape(experts, capacity, w_down.shape[1]), 'e...  9.95 us
  transfers between devices with their start and end apart: 3, of which 3 were waited for; matrix products, arithmetic and copies ran while one was open for 0% of the time, Pallas kernels for 0%

commit v1 on v0

v1 whole, which is shorter than its diff:
```python
import jax
import jax.numpy as jnp
from jax import lax
from jax.sharding import Mesh, PartitionSpec as P

BF = jnp.bfloat16
F32 = jnp.float32
CAP = 64
AXES = ("zh", "y", "x", "z", "c")


def shift(n, d):
    return [(i, (i + d) % n) for i in range(n)]


def flip(n, d):
    return [(i, i ^ d) for i in range(n)]


def contract(a, b, da, db):
    return lax.dot_general(a, b, (((da,), (db,)), ((), ())), preferred_element_type=F32)


def in_order(high, own, other, axis):
    return jnp.where(
        high, jnp.stack([other, own], axis), jnp.stack([own, other], axis)
    )


def gather_z(v):
    z = lax.axis_index("z")
    for axis, step in enumerate((4, 2, 1)):
        other = lax.ppermute(v, "z", flip(8, step))
        v = in_order((z & step) != 0, v, other, axis)
    return v.reshape(-1, v.shape[-1])


def with_other_core(v, rows):
    other = lax.ppermute(v, "c", flip(2, 1))
    lanes = v.shape[-1]
    both = in_order(
        lax.axis_index("c") != 0, v.reshape(-1, rows, lanes), other.reshape(-1, rows, lanes), 1
    )
    return both.reshape(-1, lanes)


def route(expert_ids):
    ids = expert_ids.T
    expert = lax.broadcasted_iota(jnp.int32, (8, ids.shape[1]), 0)
    first = ids[0][None, :] == expert
    second = ids[1][None, :] == expert
    ones = first.astype(BF) + second.astype(BF)
    n = ids.shape[1]
    before = lax.broadcasted_iota(jnp.int32, (n, n), 0) < lax.broadcasted_iota(jnp.int32, (n, n), 1)
    earlier = contract(ones, before.astype(BF), 1, 0)
    targets = []
    for k, (mine, count) in enumerate(((first, earlier), (second, earlier + first.astype(F32)))):
        slot = jnp.sum(jnp.where(mine, count, 0.0), axis=0).astype(jnp.int32)
        targets.append(jnp.where(slot < CAP, ids[k] * CAP + slot, -1))
    return targets


def local(tokens, expert_ids, routing_weights, gate_weight, up_weight, down_weight):
    zh, x = lax.axis_index("zh"), lax.axis_index("x")
    feats = tokens.shape[1]
    down = down_weight[0].T.reshape(feats, 4, -1)
    downs = []
    for d in range(4):
        part = lax.dynamic_index_in_dim(down, (x + d) % 4, 1, keepdims=False)
        downs.append(lax.ppermute(part, "x", shift(4, d)) if d else part)

    targets = route(expert_ids)
    slot = lax.broadcasted_iota(jnp.int32, (4 * CAP, tokens.shape[0]), 0)
    hits = []
    for half in range(2):
        base = jnp.where(half == 0, zh, 1 - zh) * (4 * CAP)
        hits.append([(t[None, :] - base) == slot for t in targets])
    packed = [contract(tokens, (a | b).astype(BF), 0, 1).astype(BF) for a, b in hits]
    packed[1] = lax.ppermute(packed[1], "zh", flip(2, 1))

    gate_up = jnp.concatenate([gate_weight[0], up_weight[0]], axis=1).reshape(4, -1, 256)
    gate_ups = [lax.dynamic_index_in_dim(gate_up, (x - d) % 4, 0, keepdims=False) for d in range(4)]

    backs = [None, None]
    for half in (0, 1):
        v = lax.all_to_all(packed[half].reshape(feats, 4, CAP), "y", 1, 0)
        v = v.transpose(1, 0, 2).reshape(feats, 4 * CAP)
        v = gather_z(v)
        both = 0.0
        for d in (0, 1, 3, 2):
            piece = lax.ppermute(v, "x", shift(4, d)) if d else v
            piece = with_other_core(piece, feats)
            both = both + contract(gate_ups[d], piece, 0, 0)
        gate, up = both[:128], both[128:]
        hidden = (jax.nn.silu(gate) * up).astype(BF)
        hidden = with_other_core(gather_z(hidden), 128)
        total = 0.0
        for d in (2, 1, 3, 0):
            part = contract(downs[d], hidden, 1, 0)
            if d:
                part = lax.ppermute(part.astype(BF), "x", shift(4, -d)).astype(F32)
            total = total + part
        out = total.astype(BF)
        back = lax.all_to_all(out.reshape(feats, 4, CAP), "y", 1, 0)
        back = back.transpose(1, 0, 2).reshape(feats, 4 * CAP)
        backs[half] = lax.ppermute(back, "zh", flip(2, 1)) if half else back

    mixed = 0.0
    for k in range(2):
        picked = sum(contract(backs[h], hits[h][k].astype(BF), 1, 0) for h in range(2))
        mixed = mixed + picked * routing_weights[:, k][None, :]
    return mixed.astype(BF).T


def solution(mesh):
    fine = Mesh(mesh.devices.reshape(2, 4, 4, 8, 2), AXES)
    rows, cols = ("zh", "y"), ("x", "z", "c")
    placed = (
        P(rows, cols),
        P(rows, None),
        P(rows, None),
        P(rows, None, cols),
        P(rows, None, cols),
        P(rows, None, cols),
    )
    return jax.shard_map(local, mesh=fine, in_specs=placed, out_specs=P(rows, cols), check_vma=False)
```

time: 352 us -> 254 us (0.72)
  the two profiles are of different devices: /device:TPU:38 before, /device:TPU:4 now
where the time goes in v1:
time: 254 us; the launch traced here: 252 us
  starting transfers between devices  146 us (57%)
  waiting for transfers between devices  55.1 us (22%)
  local copies, waits for them, and re-layouts  25.2 us (10%)
  other arithmetic  16.1 us (6%)
  matrix products  7.95 us (3%)
    ppermute x12, starting transfers between devices, gather_z(): other = lax.ppermute(v, 'z', flip(8, step))  37.4 us
    ppermute x12, waiting for transfers between devices, gather_z(): other = lax.ppermute(v, 'z', flip(8, step))  32.4 us
    ppermute x6, starting transfers between devices, local(): part = lax.ppermute(part.astype(BF), 'x', shift(4, -d)).astype(F32)  21.6 us
    ppermute x10, starting transfers between devices, with_other_core(): other = lax.ppermute(v, 'c', flip(2, 1))  20.5 us
    ppermute x6, starting transfers between devices, local(): piece = lax.ppermute(v, 'x', shift(4, d)) if d else v  20.2 us
    ppermute x1, starting transfers between devices, local(): packed[1] = lax.ppermute(packed[1], 'zh', flip(2, 1))  15.7 us
    select_n x29, other arithmetic, in_order(): jnp.where(high, jnp.stack([other, own], axis), jnp.stack([own, other], ax...  14 us
    ppermute x1, waiting for transfers between devices, local(): backs[half] = lax.ppermute(back, 'zh', flip(2, 1)) if half else back  11.3 us
  transfers between devices with their start and end apart: 43, of which 12 were waited for; matrix products, arithmetic and copies ran while one was open for 18% of the time, Pallas kernels for 0%

profile of v1, /device:TPU:4, one launch (start us, length us, event | category | flops | bytes accessed | tf_op | source)
XLA Modules:
  0.0 251.9 jit_solution(4824422671361705261)
XLA Ops:
  2.7 4.5 %all-to-all-start = ((bf16[1,96,4,64]{1,3,0,2:T(8,128)(2,1)}), bf16[1,96,4,64]{1,3,0,2:T(8,128)(2,1)S(1)}, u32[]{:S(2)}, u32[]{:S(2)}) async-start(bf16[1,96,4,64]{1,3,0,2:T(8,128)(2,1)} %bitcast.14), calls=%async_computation | async-start | bytes 131072 | tf_op jit(solution)/shard_map/all_to_all | solution.py:86
  7.3 15.7 %collective-permute-start.20 = (bf16[96,256]{1,0:T(8,128)(2,1)S(1)}, bf16[96,256]{1,0:T(8,128)(2,1)S(1)}, u32[]{:S(2)}, u32[]{:S(2)}) collective-permute-start(bf16[96,256]{1,0:T(8,128)(2,1)S(1)} %fusion.5), channel_id=1, source_target_pairs={{0,256},{256,0},{1,257},{257,1},{2,258},{258,2},{3,259},{259,3},{4... | collective-permute-start | bytes 147464 | tf_op jit(solution)/shard_map/ppermute | solution.py:79
  23.1 3.9 %reshape.994 = bf16[96,4,2048]{2,1,0:T(4,128)(2,1)} reshape(bf16[96,8192]{1,0:T(8,128)(2,1)} %bitcast.261) | data formatting | bytes 3145728 | tf_op jit(solution)/shard_map/reshape | solution.py:66
  27.0 7.3 %constant_dynamic-slice_fusion.3 = (bf16[96,1,2048]{2,1,0:T(2,128)(2,1)}, bf16[96,1,2048]{2,1,0:T(2,128)(2,1)}, bf16[96,1,2048]{2,1,0:T(2,128)(2,1)}, bf16[96,1,2048]{2,1,0:T(2,128)(2,1)}) fusion(bf16[96,4,2048]{2,1,0:T(4,128)(2,1)} %reshape.994, s32[]{:T(128)S(6)} %select_n.475, s32[]{:T(128)S(6)} %select_n.481, s32[]{:T(128)S(6)} %select_n.525, ...), kind=kLoop, calls=%fused_computation.119 | loop fusion | bytes 3145744 | tf_op jit(solution)/shard_map/jit(dynamic_index_in_dim)/dynamic_slice | solution.py:69
  34.3 4.3 %collective-permute-start.1 = (bf16[96,256]{0,1:T(8,128)(2,1)S(1)}, bf16[96,256]{0,1:T(8,128)(2,1)S(1)}, u32[]{:S(2)}, u32[]{:S(2)}) collective-permute-start(bf16[96,256]{0,1:T(8,128)(2,1)S(1)} %bitcast.280), channel_id=1, source_target_pairs={{0,8},{2,10},{4,12},{6,14},{8,0},{10,2},{12,4},{14,6},{1,9},{3,11}... | collective-permute-start | bytes 147464 | tf_op jit(solution)/shard_map/ppermute | solution.py:33
  45.5 4.8 %all-to-all-start.2 = ((bf16[1,96,4,64]{1,3,0,2:T(8,128)(2,1)}), bf16[1,96,4,64]{1,3,0,2:T(8,128)(2,1)S(1)}, u32[]{:S(2)}, u32[]{:S(2)}) async-start(bf16[1,96,4,64]{1,3,0,2:T(8,128)(2,1)} %bitcast.78), calls=%async_computation.2 | async-start | bytes 131072 | tf_op jit(solution)/shard_map/all_to_all | solution.py:86
  51.0 3.4 %collective-permute-start.2 = (bf16[2,96,256]{1,2,0:T(8,128)(2,1)}, bf16[2,96,256]{1,2,0:T(8,128)(2,1)}, u32[]{:S(2)}, u32[]{:S(2)}) collective-permute-start(bf16[2,96,256]{1,2,0:T(8,128)(2,1)} %maximum_select_fusion.22), channel_id=1, source_target_pairs={{0,4},{2,6},{4,0},{6,2},{8,12},{10,14},{12,8},{14,10},{1,5},{3,7},... | collective-permute-start | bytes 294920 | tf_op jit(solution)/shard_map/ppermute | solution.py:33
  56.0 5.4 %collective-permute-start.21 = (bf16[96,256]{0,1:T(8,128)(2,1)S(1)}, bf16[96,256]{0,1:T(8,128)(2,1)S(1)}, u32[]{:S(2)}, u32[]{:S(2)}) collective-permute-start(bf16[96,256]{0,1:T(8,128)(2,1)S(1)} %bitcast.272), channel_id=1, source_target_pairs={{0,8},{2,10},{4,12},{6,14},{8,0},{10,2},{12,4},{14,6},{1,9},{3,11}... | collective-permute-start | bytes 147464 | tf_op jit(solution)/shard_map/ppermute | solution.py:33
  61.5 6.6 %collective-permute-done.21 = bf16[96,256]{0,1:T(8,128)(2,1)S(1)} collective-permute-done((bf16[96,256]{0,1:T(8,128)(2,1)S(1)}, bf16[96,256]{0,1:T(8,128)(2,1)S(1)}, u32[]{:S(2)}, u32[]{:S(2)}) %collective-permute-start.21) | collective-permute-done | bytes 49184 | tf_op jit(solution)/shard_map/ppermute | solution.py:33
  76.1 4.5 %collective-permute-done.3 = bf16[2,2,96,256]{2,3,0,1:T(8,128)(2,1)S(1)} collective-permute-done((bf16[2,2,96,256]{2,3,0,1:T(8,128)(2,1)S(1)}, bf16[2,2,96,256]{2,3,0,1:T(8,128)(2,1)S(1)}, u32[]{:S(2)}, u32[]{:S(2)}) %collective-permute-start.3) | collective-permute-done | bytes 196640 | tf_op jit(solution)/shard_map/ppermute | solution.py:33
  88.8 3.1 %collective-permute-start.5 = (bf16[768,256]{1,0:T(8,128)(2,1)}, bf16[768,256]{1,0:T(8,128)(2,1)}, u32[]{:S(2)}, u32[]{:S(2)}) collective-permute-start(bf16[768,256]{1,0:T(8,128)(2,1)} %bitcast.268), channel_id=1, source_target_pairs={{0,16},{16,32},{32,48},{48,0},{1,17},{17,33},{33,49},{49,1},{2,18}... | collective-permute-start | bytes 1179656 | tf_op jit(solution)/shard_map/ppermute | solution.py:91
  94.8 3.6 %collective-permute-start.9 = (bf16[768,256]{1,0:T(8,128)(2,1)}, bf16[768,256]{1,0:T(8,128)(2,1)}, u32[]{:S(2)}, u32[]{:S(2)}) collective-permute-start(bf16[768,256]{1,0:T(8,128)(2,1)} %bitcast.270), channel_id=1, source_target_pairs={{0,32},{16,48},{32,0},{48,16},{1,33},{17,49},{33,1},{49,17},{2,34}... | collective-permute-start | bytes 1179656 | tf_op jit(solution)/shard_map/ppermute | solution.py:91
  103.4 2.8 %collective-permute-start.25 = (bf16[768,256]{1,0:T(8,128)(2,1)}, bf16[768,256]{1,0:T(8,128)(2,1)S(1)}, u32[]{:S(2)}, u32[]{:S(2)}) collective-permute-start(bf16[768,256]{1,0:T(8,128)(2,1)} %bitcast.263), channel_id=1, source_target_pairs={{0,16},{16,32},{32,48},{48,0},{1,17},{17,33},{33,49},{49,1},{2,18}... | collective-permute-start | bytes 1179656 | tf_op jit(solution)/shard_map/ppermute | solution.py:91
  110.5 3.1 %collective-permute-start.27 = (bf16[768,256]{1,0:T(8,128)(2,1)S(1)}, bf16[768,256]{1,0:T(8,128)(2,1)S(1)}, u32[]{:S(2)}, u32[]{:S(2)}) collective-permute-start(bf16[768,256]{1,0:T(8,128)(2,1)S(1)} %bitcast.264), channel_id=1, source_target_pairs={{0,48},{16,0},{32,16},{48,32},{1,49},{17,1},{33,17},{49,33},{2,50}... | collective-permute-start | bytes 1179656 | tf_op jit(solution)/shard_map/ppermute | solution.py:91
  113.8 4.9 %collective-permute-start.29 = (bf16[768,256]{1,0:T(8,128)(2,1)S(1)}, bf16[768,256]{1,0:T(8,128)(2,1)S(1)}, u32[]{:S(2)}, u32[]{:S(2)}) collective-permute-start(bf16[768,256]{1,0:T(8,128)(2,1)S(1)} %bitcast.266), channel_id=1, source_target_pairs={{0,32},{16,48},{32,0},{48,16},{1,33},{17,49},{33,1},{49,17},{2,34}... | collective-permute-start | bytes 1179656 | tf_op jit(solution)/shard_map/ppermute | solution.py:91
  128.3 3.9 %collective-permute-start.16 = (bf16[96,2048]{1,0:T(8,128)(2,1)S(1)}, bf16[96,2048]{1,0:T(8,128)(2,1)S(1)}, u32[]{:S(2)}, u32[]{:S(2)}) collective-permute-start(bf16[96,2048]{1,0:T(8,128)(2,1)S(1)} %bitcast.299), channel_id=1, source_target_pairs={{0,16},{16,32},{32,48},{48,0},{1,17},{17,33},{33,49},{49,1},{2,18}... | collective-permute-start | bytes 1179656 | tf_op jit(solution)/shard_map/ppermute | solution.py:70
  141.6 4.0 %collective-permute-start = (bf16[96,2048]{1,0:T(8,128)(2,1)S(1)}, bf16[96,2048]{1,0:T(8,128)(2,1)S(1)}, u32[]{:S(2)}, u32[]{:S(2)}) collective-permute-start(bf16[96,2048]{1,0:T(8,128)(2,1)S(1)} %bitcast.297), channel_id=1, source_target_pairs={{0,32},{16,48},{32,0},{48,16},{1,33},{17,49},{33,1},{49,17},{2,34}... | collective-permute-start | bytes 1179656 | tf_op jit(solution)/shard_map/ppermute | solution.py:70
  145.7 7.3 %collective-permute-start.11 = (bf16[128,256]{1,0:T(8,128)(2,1)S(1)}, bf16[128,256]{1,0:T(8,128)(2,1)S(1)}, u32[]{:S(2)}, u32[]{:S(2)}) collective-permute-start(bf16[128,256]{1,0:T(8,128)(2,1)S(1)} %fusion.28), channel_id=1, source_target_pairs={{0,8},{2,10},{4,12},{6,14},{8,0},{10,2},{12,4},{14,6},{1,9},{3,11}... | collective-permute-start | bytes 196616 | tf_op jit(solution)/shard_map/ppermute | solution.py:33
  162.1 6.6 %collective-permute-done.31 = bf16[128,256]{1,0:T(8,128)(2,1)S(1)} collective-permute-done((bf16[128,256]{1,0:T(8,128)(2,1)S(1)}, bf16[128,256]{1,0:T(8,128)(2,1)S(1)}, u32[]{:S(2)}, u32[]{:S(2)}) %collective-permute-start.31) | collective-permute-done | bytes 65568 | tf_op jit(solution)/shard_map/ppermute | solution.py:33
  174.0 4.2 %collective-permute-done.32 = bf16[2,128,256]{2,1,0:T(8,128)(2,1)S(1)} collective-permute-done((bf16[2,128,256]{2,1,0:T(8,128)(2,1)S(1)}, bf16[2,128,256]{2,1,0:T(8,128)(2,1)S(1)}, u32[]{:S(2)}, u32[]{:S(2)}) %collective-permute-start.32) | collective-permute-done | bytes 131104 | tf_op jit(solution)/shard_map/ppermute | solution.py:33
  180.2 3.7 %collective-permute-done.13 = bf16[2,2,128,256]{3,2,0,1:T(8,128)(2,1)S(1)} collective-permute-done((bf16[2,2,128,256]{3,2,0,1:T(8,128)(2,1)S(1)}, bf16[2,2,128,256]{3,2,0,1:T(8,128)(2,1)S(1)}, u32[]{:S(2)}, u32[]{:S(2)}) %collective-permute-start.13) | collective-permute-done | bytes 262176 | tf_op jit(solution)/shard_map/ppermute | solution.py:33
  186.1 2.9 %collective-permute-done.33 = bf16[2,2,128,256]{3,2,0,1:T(8,128)(2,1)S(1)} collective-permute-done((bf16[2,2,128,256]{3,2,0,1:T(8,128)(2,1)S(1)}, bf16[2,2,128,256]{3,2,0,1:T(8,128)(2,1)S(1)}, u32[]{:S(2)}, u32[]{:S(2)}) %collective-permute-start.33) | collective-permute-done | bytes 262176 | tf_op jit(solution)/shard_map/ppermute | solution.py:33
  191.6 4.5 %collective-permute-start.19 = (bf16[96,256]{1,0:T(8,128)(2,1)S(1)}, bf16[96,256]{1,0:T(8,128)(2,1)S(1)}, u32[]{:S(2)}, u32[]{:S(2)}) collective-permute-start(bf16[96,256]{1,0:T(8,128)(2,1)S(1)} %convolution_convert_fusion.3), channel_id=1, source_target_pairs={{0,16},{16,32},{32,48},{48,0},{1,17},{17,33},{33,49},{49,1},{2,18}... | collective-permute-start | bytes 147464 | tf_op jit(solution)/shard_map/ppermute | solution.py:101
  199.4 3.4 %collective-permute-start.15 = (bf16[96,256]{1,0:T(8,128)(2,1)S(1)}, bf16[96,256]{1,0:T(8,128)(2,1)S(1)}, u32[]{:S(2)}, u32[]{:S(2)}) collective-permute-start(bf16[96,256]{1,0:T(8,128)(2,1)S(1)} %convolution_convert_fusion.5), channel_id=1, source_target_pairs={{0,32},{16,48},{32,0},{48,16},{1,33},{17,49},{33,1},{49,17},{2,34}... | collective-permute-start | bytes 147464 | tf_op jit(solution)/shard_map/ppermute | solution.py:101
  203.4 4.7 %collective-permute-start.37 = (bf16[96,256]{1,0:T(8,128)(2,1)S(1)}, bf16[96,256]{1,0:T(8,128)(2,1)S(1)}, u32[]{:S(2)}, u32[]{:S(2)}) collective-permute-start(bf16[96,256]{1,0:T(8,128)(2,1)S(1)} %convolution_convert_fusion), channel_id=1, source_target_pairs={{0,16},{16,32},{32,48},{48,0},{1,17},{17,33},{33,49},{49,1},{2,18}... | collective-permute-start | bytes 147464 | tf_op jit(solution)/shard_map/ppermute | solution.py:101
  210.6 4.6 %collective-permute-start.35 = (bf16[96,256]{1,0:T(8,128)(2,1)S(1)}, bf16[96,256]{1,0:T(8,128)(2,1)S(1)}, u32[]{:S(2)}, u32[]{:S(2)}) collective-permute-start(bf16[96,256]{1,0:T(8,128)(2,1)S(1)} %convolution_convert_fusion.2), channel_id=1, source_target_pairs={{0,32},{16,48},{32,0},{48,16},{1,33},{17,49},{33,1},{49,17},{2,34}... | collective-permute-start | bytes 147464 | tf_op jit(solution)/shard_map/ppermute | solution.py:101
  216.3 4.3 %all-to-all-start.1 = ((bf16[1,96,4,64]{1,3,0,2:T(8,128)(2,1)}), bf16[1,96,4,64]{1,3,0,2:T(8,128)(2,1)S(1)}, u32[]{:S(2)}, u32[]{:S(2)}) async-start(bf16[1,96,4,64]{1,3,0,2:T(8,128)(2,1)} %bitcast.68), calls=%async_computation.1 | async-start | bytes 131072 | tf_op jit(solution)/shard_map/all_to_all | solution.py:104
  221.8 4.5 %all-to-all-done.1 = bf16[1,96,4,64]{1,3,0,2:T(8,128)(2,1)S(1)} async-done(((bf16[1,96,4,64]{1,3,0,2:T(8,128)(2,1)}), bf16[1,96,4,64]{1,3,0,2:T(8,128)(2,1)S(1)}, u32[]{:S(2)}, u32[]{:S(2)}) %all-to-all-start.1) | async-done | bytes 49184 | tf_op jit(solution)/shard_map/all_to_all | solution.py:104
  226.3 3.3 %all-to-all-start.3 = ((bf16[1,96,4,64]{1,3,0,2:T(8,128)(2,1)}), bf16[1,96,4,64]{1,3,0,2:T(8,128)(2,1)S(1)}, u32[]{:S(2)}, u32[]{:S(2)}) async-start(bf16[1,96,4,64]{1,3,0,2:T(8,128)(2,1)} %bitcast.125), calls=%async_computation.3 | async-start | bytes 131072 | tf_op jit(solution)/shard_map/all_to_all | solution.py:104
  229.8 5.4 %all-to-all-done.3 = bf16[1,96,4,64]{1,3,0,2:T(8,128)(2,1)S(1)} async-done(((bf16[1,96,4,64]{1,3,0,2:T(8,128)(2,1)}), bf16[1,96,4,64]{1,3,0,2:T(8,128)(2,1)S(1)}, u32[]{:S(2)}, u32[]{:S(2)}) %all-to-all-start.3) | async-done | bytes 49184 | tf_op jit(solution)/shard_map/all_to_all | solution.py:104
  235.1 4.2 %collective-permute-start.38 = (bf16[96,256]{0,1:T(8,128)(2,1)S(1)}, bf16[96,256]{0,1:T(8,128)(2,1)S(1)}, u32[]{:S(2)}, u32[]{:S(2)}) collective-permute-start(bf16[96,256]{0,1:T(8,128)(2,1)S(1)} %bitcast.318), channel_id=1, source_target_pairs={{0,256},{256,0},{1,257},{257,1},{2,258},{258,2},{3,259},{259,3},{4... | collective-permute-start | bytes 147464 | tf_op jit(solution)/shard_map/ppermute | solution.py:106
  239.6 11.3 %collective-permute-done.38 = bf16[96,256]{0,1:T(8,128)(2,1)S(1)} collective-permute-done((bf16[96,256]{0,1:T(8,128)(2,1)S(1)}, bf16[96,256]{0,1:T(8,128)(2,1)S(1)}, u32[]{:S(2)}, u32[]{:S(2)}) %collective-permute-start.38) | collective-permute-done | bytes 49184 | tf_op jit(solution)/shard_map/ppermute | solution.py:106
  (166 shorter events, 90.0 us)
Async XLA Ops:
  2.7 31.6 %all-to-all-start = ((bf16[1,96,4,64]{1,3,0,2:T(8,128)(2,1)}), bf16[1,96,4,64]{1,3,0,2:T(8,128)(2,1)S(1)}, u32[]{:S(2)}, u32[]{:S(2)}) async-start(bf16[1,96,4,64]{1,3,0,2:T(8,128)(2,1)} %bitcast.14), calls=%async_computation | async-start | bytes 131072 | tf_op jit(solution)/shard_map/all_to_all | solution.py:86
  7.3 37.5 %collective-permute-start.20 = (bf16[96,256]{1,0:T(8,128)(2,1)S(1)}, bf16[96,256]{1,0:T(8,128)(2,1)S(1)}, u32[]{:S(2)}, u32[]{:S(2)}) collective-permute-start(bf16[96,256]{1,0:T(8,128)(2,1)S(1)} %fusion.5), channel_id=1, source_target_pairs={{0,256},{256,0},{1,257},{257,1},{2,258},{258,2},{3,259},{259,3},{4... | collective-permute-start | bytes 147464 | tf_op jit(solution)/shard_map/ppermute | solution.py:79
  34.3 16.1 %collective-permute-start.1 = (bf16[96,256]{0,1:T(8,128)(2,1)S(1)}, bf16[96,256]{0,1:T(8,128)(2,1)S(1)}, u32[]{:S(2)}, u32[]{:S(2)}) collective-permute-start(bf16[96,256]{0,1:T(8,128)(2,1)S(1)} %bitcast.280), channel_id=1, source_target_pairs={{0,8},{2,10},{4,12},{6,14},{8,0},{10,2},{12,4},{14,6},{1,9},{3,11}... | collective-permute-start | bytes 147464 | tf_op jit(solution)/shard_map/ppermute | solution.py:33
  51.0 19.9 %collective-permute-start.2 = (bf16[2,96,256]{1,2,0:T(8,128)(2,1)}, bf16[2,96,256]{1,2,0:T(8,128)(2,1)}, u32[]{:S(2)}, u32[]{:S(2)}) collective-permute-start(bf16[2,96,256]{1,2,0:T(8,128)(2,1)} %maximum_select_fusion.22), channel_id=1, source_target_pairs={{0,4},{2,6},{4,0},{6,2},{8,12},{10,14},{12,8},{14,10},{1,5},{3,7},... | collective-permute-start | bytes 294920 | tf_op jit(solution)/shard_map/ppermute | solution.py:33
  56.0 12.2 %collective-permute-start.21 = (bf16[96,256]{0,1:T(8,128)(2,1)S(1)}, bf16[96,256]{0,1:T(8,128)(2,1)S(1)}, u32[]{:S(2)}, u32[]{:S(2)}) collective-permute-start(bf16[96,256]{0,1:T(8,128)(2,1)S(1)} %bitcast.272), channel_id=1, source_target_pairs={{0,8},{2,10},{4,12},{6,14},{8,0},{10,2},{12,4},{14,6},{1,9},{3,11}... | collective-permute-start | bytes 147464 | tf_op jit(solution)/shard_map/ppermute | solution.py:33
  68.8 16.7 %collective-permute-start.22 = (bf16[2,96,256]{1,2,0:T(8,128)(2,1)}, bf16[2,96,256]{1,2,0:T(8,128)(2,1)S(1)}, u32[]{:S(2)}, u32[]{:S(2)}) collective-permute-start(bf16[2,96,256]{1,2,0:T(8,128)(2,1)} %maximum_select_fusion.24), channel_id=1, source_target_pairs={{0,4},{2,6},{4,0},{6,2},{8,12},{10,14},{12,8},{14,10},{1,5},{3,7},... | collective-permute-start | bytes 294920 | tf_op jit(solution)/shard_map/ppermute | solution.py:33
  83.6 19.8 %collective-permute-start.4 = (bf16[768,256]{1,0:T(8,128)(2,1)}, bf16[768,256]{1,0:T(8,128)(2,1)}, u32[]{:S(2)}, u32[]{:S(2)}) collective-permute-start(bf16[768,256]{1,0:T(8,128)(2,1)} %bitcast.267), channel_id=1, source_target_pairs={{0,1},{1,0},{2,3},{3,2},{4,5},{5,4},{6,7},{7,6},{8,9},{9,8},{10,11... | collective-permute-start | bytes 1179656 | tf_op jit(solution)/shard_map/ppermute | solution.py:39
  86.6 11.9 %collective-permute-start.23 = (bf16[2,2,96,256]{2,3,0,1:T(8,128)(2,1)S(1)}, bf16[2,2,96,256]{2,3,0,1:T(8,128)(2,1)S(1)}, u32[]{:S(2)}, u32[]{:S(2)}) collective-permute-start(bf16[2,2,96,256]{2,3,0,1:T(8,128)(2,1)S(1)} %maximum_select_fusion.18), channel_id=1, source_target_pairs={{0,2},{2,0},{4,6},{6,4},{8,10},{10,8},{12,14},{14,12},{1,3},{3,1},... | collective-permute-start | bytes 589832 | tf_op jit(solution)/shard_map/ppermute | solution.py:33
  88.8 19.0 %collective-permute-start.5 = (bf16[768,256]{1,0:T(8,128)(2,1)}, bf16[768,256]{1,0:T(8,128)(2,1)}, u32[]{:S(2)}, u32[]{:S(2)}) collective-permute-start(bf16[768,256]{1,0:T(8,128)(2,1)} %bitcast.268), channel_id=1, source_target_pairs={{0,16},{16,32},{32,48},{48,0},{1,17},{17,33},{33,49},{49,1},{2,18}... | collective-permute-start | bytes 1179656 | tf_op jit(solution)/shard_map/ppermute | solution.py:91
  92.1 21.7 %collective-permute-start.7 = (bf16[768,256]{1,0:T(8,128)(2,1)}, bf16[768,256]{1,0:T(8,128)(2,1)}, u32[]{:S(2)}, u32[]{:S(2)}) collective-permute-start(bf16[768,256]{1,0:T(8,128)(2,1)} %bitcast.269), channel_id=1, source_target_pairs={{0,48},{16,0},{32,16},{48,32},{1,49},{17,1},{33,17},{49,33},{2,50}... | collective-permute-start | bytes 1179656 | tf_op jit(solution)/shard_map/ppermute | solution.py:91
  94.8 23.9 %collective-permute-start.9 = (bf16[768,256]{1,0:T(8,128)(2,1)}, bf16[768,256]{1,0:T(8,128)(2,1)}, u32[]{:S(2)}, u32[]{:S(2)}) collective-permute-start(bf16[768,256]{1,0:T(8,128)(2,1)} %bitcast.270), channel_id=1, source_target_pairs={{0,32},{16,48},{32,0},{48,16},{1,33},{17,49},{33,1},{49,17},{2,34}... | collective-permute-start | bytes 1179656 | tf_op jit(solution)/shard_map/ppermute | solution.py:91
  103.4 24.9 %collective-permute-start.25 = (bf16[768,256]{1,0:T(8,128)(2,1)}, bf16[768,256]{1,0:T(8,128)(2,1)S(1)}, u32[]{:S(2)}, u32[]{:S(2)}) collective-permute-start(bf16[768,256]{1,0:T(8,128)(2,1)} %bitcast.263), channel_id=1, source_target_pairs={{0,16},{16,32},{32,48},{48,0},{1,17},{17,33},{33,49},{49,1},{2,18}... | collective-permute-start | bytes 1179656 | tf_op jit(solution)/shard_map/ppermute | solution.py:91
  107.8 12.9 %collective-permute-start.6 = (bf16[768,256]{1,0:T(8,128)(2,1)}, bf16[768,256]{1,0:T(8,128)(2,1)S(1)}, u32[]{:S(2)}, u32[]{:S(2)}) collective-permute-start(bf16[768,256]{1,0:T(8,128)(2,1)} %collective-permute-done.5), channel_id=1, source_target_pairs={{0,1},{1,0},{2,3},{3,2},{4,5},{5,4},{6,7},{7,6},{8,9},{9,8},{10,11... | collective-permute-start | bytes 1179656 | tf_op jit(solution)/shard_map/ppermute | solution.py:39
  110.5 21.6 %collective-permute-start.27 = (bf16[768,256]{1,0:T(8,128)(2,1)S(1)}, bf16[768,256]{1,0:T(8,128)(2,1)S(1)}, u32[]{:S(2)}, u32[]{:S(2)}) collective-permute-start(bf16[768,256]{1,0:T(8,128)(2,1)S(1)} %bitcast.264), channel_id=1, source_target_pairs={{0,48},{16,0},{32,16},{48,32},{1,49},{17,1},{33,17},{49,33},{2,50}... | collective-permute-start | bytes 1179656 | tf_op jit(solution)/shard_map/ppermute | solution.py:91
  113.8 20.3 %collective-permute-start.29 = (bf16[768,256]{1,0:T(8,128)(2,1)S(1)}, bf16[768,256]{1,0:T(8,128)(2,1)S(1)}, u32[]{:S(2)}, u32[]{:S(2)}) collective-permute-start(bf16[768,256]{1,0:T(8,128)(2,1)S(1)} %bitcast.266), channel_id=1, source_target_pairs={{0,32},{16,48},{32,0},{48,16},{1,33},{17,49},{33,1},{49,17},{2,34}... | collective-permute-start | bytes 1179656 | tf_op jit(solution)/shard_map/ppermute | solution.py:91
  120.7 15.8 %collective-permute-start.10 = (bf16[768,256]{1,0:T(8,128)(2,1)}, bf16[768,256]{1,0:T(8,128)(2,1)S(1)}, u32[]{:S(2)}, u32[]{:S(2)}) collective-permute-start(bf16[768,256]{1,0:T(8,128)(2,1)} %collective-permute-done.9), channel_id=1, source_target_pairs={{0,1},{1,0},{2,3},{3,2},{4,5},{5,4},{6,7},{7,6},{8,9},{9,8},{10,11... | collective-permute-start | bytes 1179656 | tf_op jit(solution)/shard_map/ppermute | solution.py:39
  124.9 66.4 %collective-permute-start.18 = (bf16[96,2048]{1,0:T(8,128)(2,1)S(1)}, bf16[96,2048]{1,0:T(8,128)(2,1)S(1)}, u32[]{:S(2)}, u32[]{:S(2)}) collective-permute-start(bf16[96,2048]{1,0:T(8,128)(2,1)S(1)} %bitcast.298), channel_id=1, source_target_pairs={{0,48},{16,0},{32,16},{48,32},{1,49},{17,1},{33,17},{49,33},{2,50}... | collective-permute-start | bytes 1179656 | tf_op jit(solution)/shard_map/ppermute | solution.py:70
  128.3 67.9 %collective-permute-start.16 = (bf16[96,2048]{1,0:T(8,128)(2,1)S(1)}, bf16[96,2048]{1,0:T(8,128)(2,1)S(1)}, u32[]{:S(2)}, u32[]{:S(2)}) collective-permute-start(bf16[96,2048]{1,0:T(8,128)(2,1)S(1)} %bitcast.299), channel_id=1, source_target_pairs={{0,16},{16,32},{32,48},{48,0},{1,17},{17,33},{33,49},{49,1},{2,18}... | collective-permute-start | bytes 1179656 | tf_op jit(solution)/shard_map/ppermute | solution.py:70
  134.1 11.6 %collective-permute-start.28 = (bf16[768,256]{1,0:T(8,128)(2,1)S(1)}, bf16[768,256]{1,0:T(8,128)(2,1)S(1)}, u32[]{:S(2)}, u32[]{:S(2)}) collective-permute-start(bf16[768,256]{1,0:T(8,128)(2,1)S(1)} %collective-permute-done.27), channel_id=1, source_target_pairs={{0,1},{1,0},{2,3},{3,2},{4,5},{5,4},{6,7},{7,6},{8,9},{9,8},{10,11... | collective-permute-start | bytes 1179656 | tf_op jit(solution)/shard_map/ppermute | solution.py:39
  136.6 16.8 %collective-permute-start.30 = (bf16[768,256]{1,0:T(8,128)(2,1)S(1)}, bf16[768,256]{1,0:T(8,128)(2,1)S(1)}, u32[]{:S(2)}, u32[]{:S(2)}) collective-permute-start(bf16[768,256]{1,0:T(8,128)(2,1)S(1)} %collective-permute-done.29), channel_id=1, source_target_pairs={{0,1},{1,0},{2,3},{3,2},{4,5},{5,4},{6,7},{7,6},{8,9},{9,8},{10,11... | collective-permute-start | bytes 1179656 | tf_op jit(solution)/shard_map/ppermute | solution.py:39
  141.6 57.4 %collective-permute-start = (bf16[96,2048]{1,0:T(8,128)(2,1)S(1)}, bf16[96,2048]{1,0:T(8,128)(2,1)S(1)}, u32[]{:S(2)}, u32[]{:S(2)}) collective-permute-start(bf16[96,2048]{1,0:T(8,128)(2,1)S(1)} %bitcast.297), channel_id=1, source_target_pairs={{0,32},{16,48},{32,0},{48,16},{1,33},{17,49},{33,1},{49,17},{2,34}... | collective-permute-start | bytes 1179656 | tf_op jit(solution)/shard_map/ppermute | solution.py:70
  145.7 14.3 %collective-permute-start.11 = (bf16[128,256]{1,0:T(8,128)(2,1)S(1)}, bf16[128,256]{1,0:T(8,128)(2,1)S(1)}, u32[]{:S(2)}, u32[]{:S(2)}) collective-permute-start(bf16[128,256]{1,0:T(8,128)(2,1)S(1)} %fusion.28), channel_id=1, source_target_pairs={{0,8},{2,10},{4,12},{6,14},{8,0},{10,2},{12,4},{14,6},{1,9},{3,11}... | collective-permute-start | bytes 196616 | tf_op jit(solution)/shard_map/ppermute | solution.py:33
  155.0 13.7 %collective-permute-start.31 = (bf16[128,256]{1,0:T(8,128)(2,1)S(1)}, bf16[128,256]{1,0:T(8,128)(2,1)S(1)}, u32[]{:S(2)}, u32[]{:S(2)}) collective-permute-start(bf16[128,256]{1,0:T(8,128)(2,1)S(1)} %fusion.27), channel_id=1, source_target_pairs={{0,8},{2,10},{4,12},{6,14},{8,0},{10,2},{12,4},{14,6},{1,9},{3,11}... | collective-permute-start | bytes 196616 | tf_op jit(solution)/shard_map/ppermute | solution.py:33
  160.0 12.0 %collective-permute-start.12 = (bf16[2,128,256]{2,1,0:T(8,128)(2,1)S(1)}, bf16[2,128,256]{2,1,0:T(8,128)(2,1)S(1)}, u32[]{:S(2)}, u32[]{:S(2)}) collective-permute-start(bf16[2,128,256]{2,1,0:T(8,128)(2,1)S(1)} %maximum_select_fusion.23), channel_id=1, source_target_pairs={{0,4},{2,6},{4,0},{6,2},{8,12},{10,14},{12,8},{14,10},{1,5},{3,7},... | collective-permute-start | bytes 393224 | tf_op jit(solution)/shard_map/ppermute | solution.py:33
  172.0 11.9 %collective-permute-start.13 = (bf16[2,2,128,256]{3,2,0,1:T(8,128)(2,1)S(1)}, bf16[2,2,128,256]{3,2,0,1:T(8,128)(2,1)S(1)}, u32[]{:S(2)}, u32[]{:S(2)}) collective-permute-start(bf16[2,2,128,256]{3,2,0,1:T(8,128)(2,1)S(1)} %maximum_select_fusion.16), channel_id=1, source_target_pairs={{0,2},{2,0},{4,6},{6,4},{8,10},{10,8},{12,14},{14,12},{1,3},{3,1},... | collective-permute-start | bytes 786440 | tf_op jit(solution)/shard_map/ppermute | solution.py:33
  189.1 13.7 %collective-permute-start.34 = (bf16[1024,256]{1,0:T(8,128)(2,1)S(1)}, bf16[1024,256]{1,0:T(8,128)(2,1)S(1)}, u32[]{:S(2)}, u32[]{:S(2)}) collective-permute-start(bf16[1024,256]{1,0:T(8,128)(2,1)S(1)} %bitcast.257), channel_id=1, source_target_pairs={{0,1},{1,0},{2,3},{3,2},{4,5},{5,4},{6,7},{7,6},{8,9},{9,8},{10,11... | collective-permute-start | bytes 1572872 | tf_op jit(solution)/shard_map/ppermute | solution.py:39
  191.6 19.0 %collective-permute-start.19 = (bf16[96,256]{1,0:T(8,128)(2,1)S(1)}, bf16[96,256]{1,0:T(8,128)(2,1)S(1)}, u32[]{:S(2)}, u32[]{:S(2)}) collective-permute-start(bf16[96,256]{1,0:T(8,128)(2,1)S(1)} %convolution_convert_fusion.3), channel_id=1, source_target_pairs={{0,16},{16,32},{32,48},{48,0},{1,17},{17,33},{33,49},{49,1},{2,18}... | collective-permute-start | bytes 147464 | tf_op jit(solution)/shard_map/ppermute | solution.py:101
  196.5 18.7 %collective-permute-start.17 = (bf16[96,256]{1,0:T(8,128)(2,1)S(1)}, bf16[96,256]{1,0:T(8,128)(2,1)S(1)}, u32[]{:S(2)}, u32[]{:S(2)}) collective-permute-start(bf16[96,256]{1,0:T(8,128)(2,1)S(1)} %convolution_convert_fusion.4), channel_id=1, source_target_pairs={{0,48},{16,0},{32,16},{48,32},{1,49},{17,1},{33,17},{49,33},{2,50}... | collective-permute-start | bytes 147464 | tf_op jit(solution)/shard_map/ppermute | solution.py:101
  199.4 15.9 %collective-permute-start.15 = (bf16[96,256]{1,0:T(8,128)(2,1)S(1)}, bf16[96,256]{1,0:T(8,128)(2,1)S(1)}, u32[]{:S(2)}, u32[]{:S(2)}) collective-permute-start(bf16[96,256]{1,0:T(8,128)(2,1)S(1)} %convolution_convert_fusion.5), channel_id=1, source_target_pairs={{0,32},{16,48},{32,0},{48,16},{1,33},{17,49},{33,1},{49,17},{2,34}... | collective-permute-start | bytes 147464 | tf_op jit(solution)/shard_map/ppermute | solution.py:101
  203.4 17.3 %collective-permute-start.37 = (bf16[96,256]{1,0:T(8,128)(2,1)S(1)}, bf16[96,256]{1,0:T(8,128)(2,1)S(1)}, u32[]{:S(2)}, u32[]{:S(2)}) collective-permute-start(bf16[96,256]{1,0:T(8,128)(2,1)S(1)} %convolution_convert_fusion), channel_id=1, source_target_pairs={{0,16},{16,32},{32,48},{48,0},{1,17},{17,33},{33,49},{49,1},{2,18}... | collective-permute-start | bytes 147464 | tf_op jit(solution)/shard_map/ppermute | solution.py:101
  208.3 12.3 %collective-permute-start.36 = (bf16[96,256]{1,0:T(8,128)(2,1)S(1)}, bf16[96,256]{1,0:T(8,128)(2,1)S(1)}, u32[]{:S(2)}, u32[]{:S(2)}) collective-permute-start(bf16[96,256]{1,0:T(8,128)(2,1)S(1)} %convolution_convert_fusion.1), channel_id=1, source_target_pairs={{0,48},{16,0},{32,16},{48,32},{1,49},{17,1},{33,17},{49,33},{2,50}... | collective-permute-start | bytes 147464 | tf_op jit(solution)/shard_map/ppermute | solution.py:101
  235.1 15.7 %collective-permute-start.38 = (bf16[96,256]{0,1:T(8,128)(2,1)S(1)}, bf16[96,256]{0,1:T(8,128)(2,1)S(1)}, u32[]{:S(2)}, u32[]{:S(2)}) collective-permute-start(bf16[96,256]{0,1:T(8,128)(2,1)S(1)} %bitcast.318), channel_id=1, source_target_pairs={{0,256},{256,0},{1,257},{257,1},{2,258},{258,2},{3,259},{259,3},{4... | collective-permute-start | bytes 147464 | tf_op jit(solution)/shard_map/ppermute | solution.py:106
  (22 other events, 160.8 us)

commit v2 on v1

v2 whole, which is shorter than its diff:
```python
import jax
import jax.numpy as jnp
from jax import lax
from jax.experimental import pallas as pl
from jax.experimental.pallas import tpu as pltpu
from jax.sharding import Mesh, PartitionSpec as P

BF = jnp.bfloat16
F32 = jnp.float32
CAP = 64
AXES = ("zh", "y", "x", "z", "c")
ORDER = (0, 4, 2, 1, 5, 3, 6, 7)
PARTS = (3, 5)


def shift(n, d):
    return [(i, (i + d) % n) for i in range(n)]


def flip(n, d):
    return [(i, i ^ d) for i in range(n)]


def contract(a, b, da, db):
    return lax.dot_general(a, b, (((da,), (db,)), ((), ())), preferred_element_type=F32)


def held(*arrays):
    return lax.optimization_barrier(arrays)


def gather_z(v):
    over = lambda a, step: lax.ppermute(a, "z", flip(8, step))
    core = lambda a: lax.ppermute(a, "c", flip(2, 1))
    rows = v.shape[0]
    b4, b2 = over(v, 4), over(v, 2)
    early = jnp.concatenate([v, b4, b2])
    b6, b153 = over(b4, 2), over(early, 1)
    early_other = core(early)
    late = jnp.concatenate([b153, b6, over(b6, 1)])
    return early, early_other, late, core(late)


def block_order():
    z, c = lax.axis_index("z"), lax.axis_index("c")
    first = [(i, j) for j in (0, 1) for i in ORDER[: PARTS[0]]]
    last = [(i, j) for j in (0, 1) for i in ORDER[PARTS[0] :]]
    return jnp.stack([(z ^ i) * 2 + (c ^ j) for i, j in first + last]).astype(jnp.int32)


def ordered(order, operands, body, blocks, out_block, out_shape):
    return pl.pallas_call(
        body,
        grid_spec=pltpu.PrefetchScalarGridSpec(
            num_scalar_prefetch=1,
            grid=(4,),
            in_specs=[pl.BlockSpec(*b) for b in blocks],
            out_specs=pl.BlockSpec(out_block, lambda p, order_ref: (p,) + (0,) * (len(out_block) - 1)),
        ),
        out_shape=out_shape,
        compiler_params=pltpu.CompilerParams(vmem_limit_bytes=16 * 2**20),
        cost_estimate=pl.CostEstimate(
            flops=0, bytes_accessed=4 * sum(a.size for a in operands), transcendentals=0
        ),
    )(order, *operands)


def ordered_gate_up(order, gate, up):
    rows = gate.shape[0] // 64

    def body(order_ref, gate_ref, up_ref, out_ref):
        for r in range(16):
            out_ref[0, r, :, :128] = gate_ref[0, order_ref[r]]
            out_ref[0, r, :, 128:] = up_ref[0, order_ref[r]]

    taken = ((1, 16, rows, 128), lambda p, order_ref: (p, 0, 0, 0))
    shape = jax.ShapeDtypeStruct((4, 16, rows, 256), gate.dtype)
    operands = [w.reshape(4, 16, rows, 128) for w in (gate, up)]
    out = ordered(order, operands, body, [taken, taken], (1, 16, rows, 256), shape)
    return out.reshape(4, 16 * rows, 256)


def ordered_down(order, down):
    feats, hidden = down.shape[0], down.shape[1] // 4

    def body(order_ref, down_ref, out_ref):
        for r in range(16):
            block = pl.ds(pl.multiple_of(order_ref[r] * 128, 128), 128)
            out_ref[0, :, r * 128 : (r + 1) * 128] = down_ref[:, block]

    taken = ((feats, hidden), lambda p, order_ref: (0, p))
    shape = jax.ShapeDtypeStruct((4, feats, hidden), down.dtype)
    return ordered(order, [down], body, [taken], (1, feats, hidden), shape)


def times_parts(w, axis, parts):
    total, at = 0.0, 0
    for part in parts:
        rows = lax.slice_in_dim(w, at, at + part.shape[0], axis=axis)
        total = total + contract(rows, part, axis, 0)
        at += part.shape[0]
    return total


def route(expert_ids):
    ids = expert_ids.T
    expert = lax.broadcasted_iota(jnp.int32, (8, ids.shape[1]), 0)
    first = ids[0][None, :] == expert
    second = ids[1][None, :] == expert
    ones = first.astype(BF) + second.astype(BF)
    n = ids.shape[1]
    before = lax.broadcasted_iota(jnp.int32, (n, n), 0) < lax.broadcasted_iota(jnp.int32, (n, n), 1)
    earlier = contract(ones, before.astype(BF), 1, 0)
    targets = []
    for k, (mine, count) in enumerate(((first, earlier), (second, earlier + first.astype(F32)))):
        slot = jnp.sum(jnp.where(mine, count, 0.0), axis=0).astype(jnp.int32)
        targets.append(jnp.where(slot < CAP, ids[k] * CAP + slot, -1))
    return targets


def local(tokens, expert_ids, routing_weights, gate_weight, up_weight, down_weight):
    zh = lax.axis_index("zh")
    feats, lanes = tokens.shape[1], 2 * CAP
    order = block_order()

    targets = route(expert_ids)
    slot = lax.broadcasted_iota(jnp.int32, (4 * CAP, tokens.shape[0]), 0)
    hits = []
    for half in range(2):
        base = jnp.where(half == 0, zh, 1 - zh) * (4 * CAP)
        hits.append([(t[None, :] - base) == slot for t in targets])
    packed = [contract(tokens, (a | b).astype(BF), 0, 1).astype(BF) for a, b in hits]
    _, gate_weight, up_weight = held(packed[1][:8], gate_weight, up_weight)
    packed[1] = lax.ppermute(packed[1], "zh", flip(2, 1))
    gate_up = ordered_gate_up(order, gate_weight[0], up_weight[0])

    v = jnp.concatenate([p.reshape(feats, 4, CAP) for p in packed], axis=2).transpose(1, 0, 2)
    v = lax.all_to_all(v, "y", 0, 0).transpose(1, 0, 2).reshape(feats, -1)
    _, gate_up, down_weight = held(v[:8, :128], gate_up, down_weight)
    gate_up = lax.all_to_all(gate_up, "x", 0, 0)
    down = ordered_down(order, down_weight[0].T)
    parts = gather_z(v)
    terms = times_parts(gate_up, 1, parts).astype(BF)
    both = jnp.sum(lax.all_to_all(terms, "x", 0, 0).astype(F32), axis=0)
    gate, up = both[:128], both[128:]
    hidden = (jax.nn.silu(gate) * up).astype(BF)

    hidden, down = held(hidden, down)
    down = lax.all_to_all(down, "x", 0, 0)
    parts = gather_z(hidden)
    terms = times_parts(down, 2, parts).astype(BF)
    terms = terms.reshape(4, feats, 4, lanes).transpose(2, 0, 1, 3).reshape(16, feats, lanes)
    terms = lax.all_to_all(terms, ("y", "x"), 0, 0).reshape(4, 4, feats, lanes)
    back = jnp.sum(terms.astype(F32), axis=1).astype(BF).transpose(1, 0, 2)
    backs = [back[:, :, :CAP].reshape(feats, -1), back[:, :, CAP:].reshape(feats, -1)]
    backs[1] = lax.ppermute(backs[1], "zh", flip(2, 1))

    mixed = 0.0
    for k in range(2):
        picked = sum(contract(backs[h], hits[h][k].astype(BF), 1, 0) for h in range(2))
        mixed = mixed + picked * routing_weights[:, k][None, :]
    return mixed.astype(BF).T


def solution(mesh):
    fine = Mesh(mesh.devices.reshape(2, 4, 4, 8, 2), AXES)
    rows, cols = ("zh", "y"), ("x", "z", "c")
    placed = (
        P(rows, cols),
        P(rows, None),
        P(rows, None),
        P(rows, None, cols),
        P(rows, None, cols),
        P(rows, None, cols),
    )
    return jax.shard_map(local, mesh=fine, in_specs=placed, out_specs=P(rows, cols), check_vma=False)
```

time: 254 us -> 185 us (0.73)
  the two profiles are of different devices: /device:TPU:4 before, /device:TPU:32 now
where the time goes in v2:
time: 185 us; the launch traced here: 184 us
  starting transfers between devices  89.1 us (48%)
  waiting for transfers between devices  69.9 us (38%)
  matrix products  13.1 us (7%)
  Pallas kernels  5.46 us (3%)
  local copies, waits for them, and re-layouts  4.57 us (2%)
    ppermute x10, starting transfers between devices, gather_z(): over = lambda a, step: lax.ppermute(a, 'z', flip(8, step))  36.3 us
    ppermute x10, waiting for transfers between devices, gather_z(): over = lambda a, step: lax.ppermute(a, 'z', flip(8, step))  31.8 us
    ppermute x1, starting transfers between devices, local(): packed[1] = lax.ppermute(packed[1], 'zh', flip(2, 1))  14.8 us
    dot_general x15, matrix products, contract(): lax.dot_general(a, b, (((da,), (db,)), ((), ())), preferred_element_type=...  13.1 us
    all_to_all x1, waiting for transfers between devices, local(): both = jnp.sum(lax.all_to_all(terms, 'x', 0, 0).astype(F32), axis=0)  12.7 us
    ppermute x1, waiting for transfers between devices, local(): backs[1] = lax.ppermute(backs[1], 'zh', flip(2, 1))  10.4 us
    all_to_all x1, waiting for transfers between devices, local(): terms = lax.all_to_all(terms, ('y', 'x'), 0, 0).reshape(4, 4, feats, lanes)  10.4 us
    ppermute x4, starting transfers between devices, gather_z(): core = lambda a: lax.ppermute(a, 'c', flip(2, 1))  8.17 us
  transfers between devices with their start and end apart: 21, of which 14 were waited for; matrix products, arithmetic and copies ran while one was open for 3% of the time, Pallas kernels for 3%

profile of v2, /device:TPU:32, one launch (start us, length us, event | category | flops | bytes accessed | tf_op | source)
XLA Modules:
  0.0 183.7 jit_solution(18371615382697236245)
XLA Ops:
  2.0 14.8 %collective-permute-start = (bf16[96,256]{1,0:T(8,128)(2,1)S(1)}, bf16[96,256]{1,0:T(8,128)(2,1)S(1)}, u32[]{:S(2)}, u32[]{:S(2)}) collective-permute-start(bf16[96,256]{1,0:T(8,128)(2,1)S(1)} %fusion.8), channel_id=1, source_target_pairs={{0,256},{256,0},{1,257},{257,1},{2,258},{258,2},{3,259},{259,3},{4... | collective-permute-start | bytes 147464 | tf_op jit(solution)/shard_map/ppermute | solution.py:134
  17.2 2.8 %collective-permute-done = bf16[96,256]{1,0:T(8,128)(2,1)S(1)} collective-permute-done((bf16[96,256]{1,0:T(8,128)(2,1)S(1)}, bf16[96,256]{1,0:T(8,128)(2,1)S(1)}, u32[]{:S(2)}, u32[]{:S(2)}) %collective-permute-start) | collective-permute-done | bytes 49184 | tf_op jit(solution)/shard_map/ppermute | solution.py:134
  20.9 4.5 %all-to-all-start.1 = ((bf16[4,96,128]{2,1,0:T(8,128)(2,1)}), bf16[4,96,128]{2,1,0:T(8,128)(2,1)S(1)}, u32[]{:S(2)}, u32[]{:S(2)}) async-start(bf16[4,96,128]{2,1,0:T(8,128)(2,1)} %copy.13), calls=%async_computation.1 | async-start | bytes 196608 | tf_op jit(solution)/shard_map/all_to_all | solution.py:138
  26.9 2.9 %shard_map.64 = bf16[4,16,96,256]{3,2,1,0:T(8,128)(2,1)} custom-call(s32[16]{0:T(128)S(1)} %stack.67.order_ref, bf16[4,16,96,128]{3,2,1,0:T(8,128)(2,1)S(1)} %bitcast.94, bf16[4,16,96,128]{3,2,1,0:T(8,128)(2,1)S(1)} %bitcast.95), custom_call_target="tpu_custom_call" | custom-call | bytes 6291456 | tf_op jit(solution)/shard_map/pallas_call | solution.py:52
  31.1 4.6 %all-to-all-start = ((bf16[4,1536,256]{2,1,0:T(8,128)(2,1)}), bf16[4,1536,256]{2,1,0:T(8,128)(2,1)}, u32[]{:S(2)}, u32[]{:S(2)}) async-start(bf16[4,1536,256]{2,1,0:T(8,128)(2,1)} %bitcast.23), calls=%async_computation | async-start | bytes 6291456 | tf_op jit(solution)/shard_map/all_to_all | solution.py:140
  35.8 5.8 %collective-permute-start.1 = (bf16[96,512]{1,0:T(8,128)(2,1)S(1)}, bf16[96,512]{1,0:T(8,128)(2,1)S(1)}, u32[]{:S(2)}, u32[]{:S(2)}) collective-permute-start(bf16[96,512]{1,0:T(8,128)(2,1)S(1)} %copy_bitcast_fusion.1), channel_id=1, source_target_pairs={{0,8},{2,10},{4,12},{6,14},{8,0},{10,2},{12,4},{14,6},{1,9},{3,11}... | collective-permute-start | bytes 294920 | tf_op jit(solution)/shard_map/ppermute | solution.py:33
  41.6 5.2 %collective-permute-start.2 = (bf16[96,512]{1,0:T(8,128)(2,1)S(1)}, bf16[96,512]{1,0:T(8,128)(2,1)S(1)}, u32[]{:S(2)}, u32[]{:S(2)}) collective-permute-start(bf16[96,512]{1,0:T(8,128)(2,1)S(1)} %copy_bitcast_fusion.1), channel_id=1, source_target_pairs={{0,4},{2,6},{4,0},{6,2},{8,12},{10,14},{12,8},{14,10},{1,5},{3,7},... | collective-permute-start | bytes 294920 | tf_op jit(solution)/shard_map/ppermute | solution.py:33
  46.8 3.1 %collective-permute-done.1 = bf16[96,512]{1,0:T(8,128)(2,1)S(1)} collective-permute-done((bf16[96,512]{1,0:T(8,128)(2,1)S(1)}, bf16[96,512]{1,0:T(8,128)(2,1)S(1)}, u32[]{:S(2)}, u32[]{:S(2)}) %collective-permute-start.1) | collective-permute-done | bytes 98336 | tf_op jit(solution)/shard_map/ppermute | solution.py:33
  50.5 4.3 %collective-permute-start.4 = (bf16[288,512]{1,0:T(8,128)(2,1)S(1)}, bf16[288,512]{1,0:T(8,128)(2,1)S(1)}, u32[]{:S(2)}, u32[]{:S(2)}) collective-permute-start(bf16[288,512]{1,0:T(8,128)(2,1)S(1)} %constant_dynamic-update-slice_fusion), channel_id=1, source_target_pairs={{0,2},{2,0},{4,6},{6,4},{8,10},{10,8},{12,14},{14,12},{1,3},{3,1},... | collective-permute-start | bytes 884744 | tf_op jit(solution)/shard_map/ppermute | solution.py:33
  54.8 3.3 %collective-permute-start.5 = (bf16[96,512]{1,0:T(8,128)(2,1)S(1)}, bf16[96,512]{1,0:T(8,128)(2,1)S(1)}, u32[]{:S(2)}, u32[]{:S(2)}) collective-permute-start(bf16[96,512]{1,0:T(8,128)(2,1)S(1)} %collective-permute-done.1), channel_id=1, source_target_pairs={{0,4},{2,6},{4,0},{6,2},{8,12},{10,14},{12,8},{14,10},{1,5},{3,7},... | collective-permute-start | bytes 294920 | tf_op jit(solution)/shard_map/ppermute | solution.py:33
  58.1 4.9 %collective-permute-done.5 = bf16[96,512]{1,0:T(8,128)(2,1)S(1)} collective-permute-done((bf16[96,512]{1,0:T(8,128)(2,1)S(1)}, bf16[96,512]{1,0:T(8,128)(2,1)S(1)}, u32[]{:S(2)}, u32[]{:S(2)}) %collective-permute-start.5) | collective-permute-done | bytes 98336 | tf_op jit(solution)/shard_map/ppermute | solution.py:33
  63.0 2.1 %collective-permute-start.6 = (bf16[96,512]{1,0:T(8,128)(2,1)S(1)}, bf16[96,512]{1,0:T(8,128)(2,1)S(1)}, u32[]{:S(2)}, u32[]{:S(2)}) collective-permute-start(bf16[96,512]{1,0:T(8,128)(2,1)S(1)} %collective-permute-done.5), channel_id=1, source_target_pairs={{0,2},{2,0},{4,6},{6,4},{8,10},{10,8},{12,14},{14,12},{1,3},{3,1},... | collective-permute-start | bytes 294920 | tf_op jit(solution)/shard_map/ppermute | solution.py:33
  65.1 4.4 %collective-permute-done.6 = bf16[96,512]{1,0:T(8,128)(2,1)S(1)} collective-permute-done((bf16[96,512]{1,0:T(8,128)(2,1)S(1)}, bf16[96,512]{1,0:T(8,128)(2,1)S(1)}, u32[]{:S(2)}, u32[]{:S(2)}) %collective-permute-start.6) | collective-permute-done | bytes 98336 | tf_op jit(solution)/shard_map/ppermute | solution.py:33
  69.5 1.9 %collective-permute-start.7 = (bf16[480,512]{1,0:T(8,128)(2,1)S(1)}, bf16[480,512]{1,0:T(8,128)(2,1)S(1)}, u32[]{:S(2)}, u32[]{:S(2)}) collective-permute-start(bf16[480,512]{1,0:T(8,128)(2,1)S(1)} %constant_dynamic-update-slice_fusion.3), channel_id=1, source_target_pairs={{0,1},{1,0},{2,3},{3,2},{4,5},{5,4},{6,7},{7,6},{8,9},{9,8},{10,11... | collective-permute-start | bytes 1474568 | tf_op jit(solution)/shard_map/ppermute | solution.py:34
  71.4 2.4 %collective-permute-start.3 = (bf16[288,512]{1,0:T(8,128)(2,1)S(1)}, bf16[288,512]{1,0:T(8,128)(2,1)S(1)}, u32[]{:S(2)}, u32[]{:S(2)}) collective-permute-start(bf16[288,512]{1,0:T(8,128)(2,1)S(1)} %constant_dynamic-update-slice_fusion), channel_id=1, source_target_pairs={{0,1},{1,0},{2,3},{3,2},{4,5},{5,4},{6,7},{7,6},{8,9},{9,8},{10,11... | collective-permute-start | bytes 884744 | tf_op jit(solution)/shard_map/ppermute | solution.py:34
  73.9 1.9 %fusion.9 = f32[4,256,512]{2,1,0:T(8,128)S(1)} fusion(bf16[4,1536,256]{2,1,0:T(8,128)(2,1)} %all-to-all-done, bf16[480,512]{1,0:T(8,128)(2,1)S(1)} %collective-permute-done.7), kind=kOutput, calls=%fused_computation.17 | convolution fusion | flops 503316480 | bytes 3571712 | tf_op jit(solution)/shard_map/dot_general | solution.py:25
  79.5 2.9 %add_convert_fusion = bf16[4,256,512]{2,1,0:T(8,128)(2,1)} fusion(f32[4,256,512]{2,1,0:T(8,128)S(1)} %fusion.9, f32[4,256,512]{2,1,0:T(8,128)S(1)} %fusion.17, f32[4,256,512]{2,1,0:T(8,128)S(1)} %fusion.15, bf16[4,1536,256]{2,1,0:T(8,128)(2,1)} %all-to-all-done, bf16[480,512]{1,0:T(8,128)(2,1)S(1)} %constant_dynamic-update-slice_fusion.3), kind=kOutput, calls=%fused_computation.1 | convolution fusion | flops 505413632 | bytes 8814592 | tf_op jit(solution)/shard_map/dot_general | solution.py:25
  82.4 4.3 %all-to-all-start.2 = ((bf16[4,256,512]{2,1,0:T(8,128)(2,1)}), bf16[4,256,512]{2,1,0:T(8,128)(2,1)S(1)}, u32[]{:S(2)}, u32[]{:S(2)}) async-start(bf16[4,256,512]{2,1,0:T(8,128)(2,1)} %add_convert_fusion), calls=%async_computation.2 | async-start | bytes 2097152 | tf_op jit(solution)/shard_map/all_to_all | solution.py:144
  86.7 2.5 %shard_map.65 = bf16[4,96,2048]{2,1,0:T(8,128)(2,1)} custom-call(s32[16]{0:T(128)S(1)} %stack.67.order_ref, bf16[96,8192]{1,0:T(8,128)(2,1)S(1)} %bitcast.96), custom_call_target="tpu_custom_call" | custom-call | bytes 3145728 | tf_op jit(solution)/shard_map/pallas_call | solution.py:52
  89.2 12.7 %all-to-all-done.2 = bf16[4,256,512]{2,1,0:T(8,128)(2,1)S(1)} async-done(((bf16[4,256,512]{2,1,0:T(8,128)(2,1)}), bf16[4,256,512]{2,1,0:T(8,128)(2,1)S(1)}, u32[]{:S(2)}, u32[]{:S(2)}) %all-to-all-start.2) | async-done | bytes 1048608 | tf_op jit(solution)/shard_map/all_to_all | solution.py:144
  102.2 6.7 %collective-permute-start.8 = (bf16[128,512]{1,0:T(8,128)(2,1)S(1)}, bf16[128,512]{1,0:T(8,128)(2,1)S(1)}, u32[]{:S(2)}, u32[]{:S(2)}) collective-permute-start(bf16[128,512]{1,0:T(8,128)(2,1)S(1)} %fusion.30), channel_id=1, source_target_pairs={{0,8},{2,10},{4,12},{6,14},{8,0},{10,2},{12,4},{14,6},{1,9},{3,11}... | collective-permute-start | bytes 393224 | tf_op jit(solution)/shard_map/ppermute | solution.py:33
  110.9 3.6 %all-to-all-start.3 = ((bf16[4,96,2048]{2,1,0:T(8,128)(2,1)}), bf16[4,96,2048]{2,1,0:T(8,128)(2,1)S(1)}, u32[]{:S(2)}, u32[]{:S(2)}) async-start(bf16[4,96,2048]{2,1,0:T(8,128)(2,1)} %shard_map.65), calls=%async_computation.3 | async-start | bytes 3145728 | tf_op jit(solution)/shard_map/all_to_all | solution.py:149
  116.4 4.4 %collective-permute-done.9 = bf16[128,512]{1,0:T(8,128)(2,1)S(1)} collective-permute-done((bf16[128,512]{1,0:T(8,128)(2,1)S(1)}, bf16[128,512]{1,0:T(8,128)(2,1)S(1)}, u32[]{:S(2)}, u32[]{:S(2)}) %collective-permute-start.9) | collective-permute-done | bytes 131104 | tf_op jit(solution)/shard_map/ppermute | solution.py:33
  122.7 3.1 %collective-permute-start.12 = (bf16[128,512]{1,0:T(8,128)(2,1)S(1)}, bf16[128,512]{1,0:T(8,128)(2,1)S(1)}, u32[]{:S(2)}, u32[]{:S(2)}) collective-permute-start(bf16[128,512]{1,0:T(8,128)(2,1)S(1)} %collective-permute-done.8), channel_id=1, source_target_pairs={{0,4},{2,6},{4,0},{6,2},{8,12},{10,14},{12,8},{14,10},{1,5},{3,7},... | collective-permute-start | bytes 393224 | tf_op jit(solution)/shard_map/ppermute | solution.py:33
  125.8 1.9 %collective-permute-start.10 = (bf16[384,512]{1,0:T(8,128)(2,1)S(1)}, bf16[384,512]{1,0:T(8,128)(2,1)}, u32[]{:S(2)}, u32[]{:S(2)}) collective-permute-start(bf16[384,512]{1,0:T(8,128)(2,1)S(1)} %constant_dynamic-update-slice_fusion.6), channel_id=1, source_target_pairs={{0,1},{1,0},{2,3},{3,2},{4,5},{5,4},{6,7},{7,6},{8,9},{9,8},{10,11... | collective-permute-start | bytes 1179656 | tf_op jit(solution)/shard_map/ppermute | solution.py:34
  127.8 7.7 %collective-permute-done.12 = bf16[128,512]{1,0:T(8,128)(2,1)S(1)} collective-permute-done((bf16[128,512]{1,0:T(8,128)(2,1)S(1)}, bf16[128,512]{1,0:T(8,128)(2,1)S(1)}, u32[]{:S(2)}, u32[]{:S(2)}) %collective-permute-start.12) | collective-permute-done | bytes 131104 | tf_op jit(solution)/shard_map/ppermute | solution.py:33
  137.5 4.9 %collective-permute-done.13 = bf16[128,512]{1,0:T(8,128)(2,1)S(1)} collective-permute-done((bf16[128,512]{1,0:T(8,128)(2,1)S(1)}, bf16[128,512]{1,0:T(8,128)(2,1)S(1)}, u32[]{:S(2)}, u32[]{:S(2)}) %collective-permute-start.13) | collective-permute-done | bytes 131104 | tf_op jit(solution)/shard_map/ppermute | solution.py:33
  142.4 1.9 %collective-permute-start.14 = (bf16[640,512]{1,0:T(8,128)(2,1)S(1)}, bf16[640,512]{1,0:T(8,128)(2,1)S(1)}, u32[]{:S(2)}, u32[]{:S(2)}) collective-permute-start(bf16[640,512]{1,0:T(8,128)(2,1)S(1)} %constant_dynamic-update-slice_fusion.9), channel_id=1, source_target_pairs={{0,1},{1,0},{2,3},{3,2},{4,5},{5,4},{6,7},{7,6},{8,9},{9,8},{10,11... | collective-permute-start | bytes 1966088 | tf_op jit(solution)/shard_map/ppermute | solution.py:34
  148.1 5.4 %all-to-all-start.4 = ((bf16[16,96,128]{2,1,0:T(8,128)(2,1)}), bf16[16,96,128]{2,1,0:T(8,128)(2,1)S(1)}, u32[]{:S(2)}, u32[]{:S(2)}) async-start(bf16[16,96,128]{2,1,0:T(8,128)(2,1)} %bitcast.45), calls=%async_computation.4 | async-start | bytes 786432 | tf_op jit(solution)/shard_map/all_to_all | solution.py:153
  153.5 10.4 %all-to-all-done.4 = bf16[16,96,128]{2,1,0:T(8,128)(2,1)S(1)} async-done(((bf16[16,96,128]{2,1,0:T(8,128)(2,1)}), bf16[16,96,128]{2,1,0:T(8,128)(2,1)S(1)}, u32[]{:S(2)}, u32[]{:S(2)}) %all-to-all-start.4) | async-done | bytes 393248 | tf_op jit(solution)/shard_map/all_to_all | solution.py:153
  164.5 7.5 %collective-permute-start.15 = (bf16[96,256]{0,1:T(8,128)(2,1)S(1)}, bf16[96,256]{0,1:T(8,128)(2,1)S(1)}, u32[]{:S(2)}, u32[]{:S(2)}) collective-permute-start(bf16[96,256]{0,1:T(8,128)(2,1)S(1)} %bitcast.102), channel_id=1, source_target_pairs={{0,256},{256,0},{1,257},{257,1},{2,258},{258,2},{3,259},{259,3},{4... | collective-permute-start | bytes 147464 | tf_op jit(solution)/shard_map/ppermute | solution.py:156
  172.2 10.4 %collective-permute-done.15 = bf16[96,256]{0,1:T(8,128)(2,1)S(1)} collective-permute-done((bf16[96,256]{0,1:T(8,128)(2,1)S(1)}, bf16[96,256]{0,1:T(8,128)(2,1)S(1)}, u32[]{:S(2)}, u32[]{:S(2)}) %collective-permute-start.15) | collective-permute-done | bytes 49184 | tf_op jit(solution)/shard_map/ppermute | solution.py:156
  (68 shorter events, 23.8 us)
Async XLA Ops:
  0.0 1.8 copy-start
  0.0 25.4 %copy-start.1 = (bf16[1,6144,128]{2,1,0:T(8,128)(2,1)S(1)}, bf16[1,6144,128]{2,1,0:T(8,128)(2,1)}, u32[]{:S(2)}) copy-start(bf16[1,6144,128]{2,1,0:T(8,128)(2,1)} %param.9) | copy-start | bytes 4718596
  2.0 18.0 %collective-permute-start = (bf16[96,256]{1,0:T(8,128)(2,1)S(1)}, bf16[96,256]{1,0:T(8,128)(2,1)S(1)}, u32[]{:S(2)}, u32[]{:S(2)}) collective-permute-start(bf16[96,256]{1,0:T(8,128)(2,1)S(1)} %fusion.8), channel_id=1, source_target_pairs={{0,256},{256,0},{1,257},{257,1},{2,258},{258,2},{3,259},{259,3},{4... | collective-permute-start | bytes 147464 | tf_op jit(solution)/shard_map/ppermute | solution.py:134
  20.9 10.3 %all-to-all-start.1 = ((bf16[4,96,128]{2,1,0:T(8,128)(2,1)}), bf16[4,96,128]{2,1,0:T(8,128)(2,1)S(1)}, u32[]{:S(2)}, u32[]{:S(2)}) async-start(bf16[4,96,128]{2,1,0:T(8,128)(2,1)} %copy.13), calls=%async_computation.1 | async-start | bytes 196608 | tf_op jit(solution)/shard_map/all_to_all | solution.py:138
  25.4 1.4 copy-start.2
  31.1 42.7 %all-to-all-start = ((bf16[4,1536,256]{2,1,0:T(8,128)(2,1)}), bf16[4,1536,256]{2,1,0:T(8,128)(2,1)}, u32[]{:S(2)}, u32[]{:S(2)}) async-start(bf16[4,1536,256]{2,1,0:T(8,128)(2,1)} %bitcast.23), calls=%async_computation | async-start | bytes 6291456 | tf_op jit(solution)/shard_map/all_to_all | solution.py:140
  35.8 14.1 %collective-permute-start.1 = (bf16[96,512]{1,0:T(8,128)(2,1)S(1)}, bf16[96,512]{1,0:T(8,128)(2,1)S(1)}, u32[]{:S(2)}, u32[]{:S(2)}) collective-permute-start(bf16[96,512]{1,0:T(8,128)(2,1)S(1)} %copy_bitcast_fusion.1), channel_id=1, source_target_pairs={{0,8},{2,10},{4,12},{6,14},{8,0},{10,2},{12,4},{14,6},{1,9},{3,11}... | collective-permute-start | bytes 294920 | tf_op jit(solution)/shard_map/ppermute | solution.py:33
  41.6 8.9 %collective-permute-start.2 = (bf16[96,512]{1,0:T(8,128)(2,1)S(1)}, bf16[96,512]{1,0:T(8,128)(2,1)S(1)}, u32[]{:S(2)}, u32[]{:S(2)}) collective-permute-start(bf16[96,512]{1,0:T(8,128)(2,1)S(1)} %copy_bitcast_fusion.1), channel_id=1, source_target_pairs={{0,4},{2,6},{4,0},{6,2},{8,12},{10,14},{12,8},{14,10},{1,5},{3,7},... | collective-permute-start | bytes 294920 | tf_op jit(solution)/shard_map/ppermute | solution.py:33
  50.5 14.5 %collective-permute-start.4 = (bf16[288,512]{1,0:T(8,128)(2,1)S(1)}, bf16[288,512]{1,0:T(8,128)(2,1)S(1)}, u32[]{:S(2)}, u32[]{:S(2)}) collective-permute-start(bf16[288,512]{1,0:T(8,128)(2,1)S(1)} %constant_dynamic-update-slice_fusion), channel_id=1, source_target_pairs={{0,2},{2,0},{4,6},{6,4},{8,10},{10,8},{12,14},{14,12},{1,3},{3,1},... | collective-permute-start | bytes 884744 | tf_op jit(solution)/shard_map/ppermute | solution.py:33
  54.8 8.2 %collective-permute-start.5 = (bf16[96,512]{1,0:T(8,128)(2,1)S(1)}, bf16[96,512]{1,0:T(8,128)(2,1)S(1)}, u32[]{:S(2)}, u32[]{:S(2)}) collective-permute-start(bf16[96,512]{1,0:T(8,128)(2,1)S(1)} %collective-permute-done.1), channel_id=1, source_target_pairs={{0,4},{2,6},{4,0},{6,2},{8,12},{10,14},{12,8},{14,10},{1,5},{3,7},... | collective-permute-start | bytes 294920 | tf_op jit(solution)/shard_map/ppermute | solution.py:33
  63.0 6.5 %collective-permute-start.6 = (bf16[96,512]{1,0:T(8,128)(2,1)S(1)}, bf16[96,512]{1,0:T(8,128)(2,1)S(1)}, u32[]{:S(2)}, u32[]{:S(2)}) collective-permute-start(bf16[96,512]{1,0:T(8,128)(2,1)S(1)} %collective-permute-done.5), channel_id=1, source_target_pairs={{0,2},{2,0},{4,6},{6,4},{8,10},{10,8},{12,14},{14,12},{1,3},{3,1},... | collective-permute-start | bytes 294920 | tf_op jit(solution)/shard_map/ppermute | solution.py:33
  69.5 4.3 %collective-permute-start.7 = (bf16[480,512]{1,0:T(8,128)(2,1)S(1)}, bf16[480,512]{1,0:T(8,128)(2,1)S(1)}, u32[]{:S(2)}, u32[]{:S(2)}) collective-permute-start(bf16[480,512]{1,0:T(8,128)(2,1)S(1)} %constant_dynamic-update-slice_fusion.3), channel_id=1, source_target_pairs={{0,1},{1,0},{2,3},{3,2},{4,5},{5,4},{6,7},{7,6},{8,9},{9,8},{10,11... | collective-permute-start | bytes 1474568 | tf_op jit(solution)/shard_map/ppermute | solution.py:34
  71.4 6.2 %collective-permute-start.3 = (bf16[288,512]{1,0:T(8,128)(2,1)S(1)}, bf16[288,512]{1,0:T(8,128)(2,1)S(1)}, u32[]{:S(2)}, u32[]{:S(2)}) collective-permute-start(bf16[288,512]{1,0:T(8,128)(2,1)S(1)} %constant_dynamic-update-slice_fusion), channel_id=1, source_target_pairs={{0,1},{1,0},{2,3},{3,2},{4,5},{5,4},{6,7},{7,6},{8,9},{9,8},{10,11... | collective-permute-start | bytes 884744 | tf_op jit(solution)/shard_map/ppermute | solution.py:34
  82.4 4.3 %copy-start.3 = (bf16[1,8192,96]{1,2,0:T(8,128)(2,1)S(1)}, bf16[1,8192,96]{1,2,0:T(8,128)(2,1)}, u32[]{:S(2)}) copy-start(bf16[1,8192,96]{1,2,0:T(8,128)(2,1)} %param.11) | copy-start | bytes 4718596
  82.4 19.6 %all-to-all-start.2 = ((bf16[4,256,512]{2,1,0:T(8,128)(2,1)}), bf16[4,256,512]{2,1,0:T(8,128)(2,1)S(1)}, u32[]{:S(2)}, u32[]{:S(2)}) async-start(bf16[4,256,512]{2,1,0:T(8,128)(2,1)} %add_convert_fusion), calls=%async_computation.2 | async-start | bytes 2097152 | tf_op jit(solution)/shard_map/all_to_all | solution.py:144
  102.2 14.1 %collective-permute-start.8 = (bf16[128,512]{1,0:T(8,128)(2,1)S(1)}, bf16[128,512]{1,0:T(8,128)(2,1)S(1)}, u32[]{:S(2)}, u32[]{:S(2)}) collective-permute-start(bf16[128,512]{1,0:T(8,128)(2,1)S(1)} %fusion.30), channel_id=1, source_target_pairs={{0,8},{2,10},{4,12},{6,14},{8,0},{10,2},{12,4},{14,6},{1,9},{3,11}... | collective-permute-start | bytes 393224 | tf_op jit(solution)/shard_map/ppermute | solution.py:33
  109.0 11.8 %collective-permute-start.9 = (bf16[128,512]{1,0:T(8,128)(2,1)S(1)}, bf16[128,512]{1,0:T(8,128)(2,1)S(1)}, u32[]{:S(2)}, u32[]{:S(2)}) collective-permute-start(bf16[128,512]{1,0:T(8,128)(2,1)S(1)} %fusion.30), channel_id=1, source_target_pairs={{0,4},{2,6},{4,0},{6,2},{8,12},{10,14},{12,8},{14,10},{1,5},{3,7},... | collective-permute-start | bytes 393224 | tf_op jit(solution)/shard_map/ppermute | solution.py:33
  110.9 33.4 %all-to-all-start.3 = ((bf16[4,96,2048]{2,1,0:T(8,128)(2,1)}), bf16[4,96,2048]{2,1,0:T(8,128)(2,1)S(1)}, u32[]{:S(2)}, u32[]{:S(2)}) async-start(bf16[4,96,2048]{2,1,0:T(8,128)(2,1)} %shard_map.65), calls=%async_computation.3 | async-start | bytes 3145728 | tf_op jit(solution)/shard_map/all_to_all | solution.py:149
  120.7 16.7 %collective-permute-start.11 = (bf16[384,512]{1,0:T(8,128)(2,1)S(1)}, bf16[384,512]{1,0:T(8,128)(2,1)S(1)}, u32[]{:S(2)}, u32[]{:S(2)}) collective-permute-start(bf16[384,512]{1,0:T(8,128)(2,1)S(1)} %constant_dynamic-update-slice_fusion.6), channel_id=1, source_target_pairs={{0,2},{2,0},{4,6},{6,4},{8,10},{10,8},{12,14},{14,12},{1,3},{3,1},... | collective-permute-start | bytes 1179656 | tf_op jit(solution)/shard_map/ppermute | solution.py:33
  122.7 12.8 %collective-permute-start.12 = (bf16[128,512]{1,0:T(8,128)(2,1)S(1)}, bf16[128,512]{1,0:T(8,128)(2,1)S(1)}, u32[]{:S(2)}, u32[]{:S(2)}) collective-permute-start(bf16[128,512]{1,0:T(8,128)(2,1)S(1)} %collective-permute-done.8), channel_id=1, source_target_pairs={{0,4},{2,6},{4,0},{6,2},{8,12},{10,14},{12,8},{14,10},{1,5},{3,7},... | collective-permute-start | bytes 393224 | tf_op jit(solution)/shard_map/ppermute | solution.py:33
  125.8 18.5 %collective-permute-start.10 = (bf16[384,512]{1,0:T(8,128)(2,1)S(1)}, bf16[384,512]{1,0:T(8,128)(2,1)}, u32[]{:S(2)}, u32[]{:S(2)}) collective-permute-start(bf16[384,512]{1,0:T(8,128)(2,1)S(1)} %constant_dynamic-update-slice_fusion.6), channel_id=1, source_target_pairs={{0,1},{1,0},{2,3},{3,2},{4,5},{5,4},{6,7},{7,6},{8,9},{9,8},{10,11... | collective-permute-start | bytes 1179656 | tf_op jit(solution)/shard_map/ppermute | solution.py:34
  135.5 6.8 %collective-permute-start.13 = (bf16[128,512]{1,0:T(8,128)(2,1)S(1)}, bf16[128,512]{1,0:T(8,128)(2,1)S(1)}, u32[]{:S(2)}, u32[]{:S(2)}) collective-permute-start(bf16[128,512]{1,0:T(8,128)(2,1)S(1)} %collective-permute-done.12), channel_id=1, source_target_pairs={{0,2},{2,0},{4,6},{6,4},{8,10},{10,8},{12,14},{14,12},{1,3},{3,1},... | collective-permute-start | bytes 393224 | tf_op jit(solution)/shard_map/ppermute | solution.py:33
  142.4 4.0 %collective-permute-start.14 = (bf16[640,512]{1,0:T(8,128)(2,1)S(1)}, bf16[640,512]{1,0:T(8,128)(2,1)S(1)}, u32[]{:S(2)}, u32[]{:S(2)}) collective-permute-start(bf16[640,512]{1,0:T(8,128)(2,1)S(1)} %constant_dynamic-update-slice_fusion.9), channel_id=1, source_target_pairs={{0,1},{1,0},{2,3},{3,2},{4,5},{5,4},{6,7},{7,6},{8,9},{9,8},{10,11... | collective-permute-start | bytes 1966088 | tf_op jit(solution)/shard_map/ppermute | solution.py:34
  146.8 6.7 %copy-start.4 = (f32[256,2]{0,1:T(2,128)S(1)}, f32[256,2]{0,1:T(2,128)}, u32[]{:S(2)}) copy-start(f32[256,2]{0,1:T(2,128)} %param.8) | copy-start | bytes 6148
  148.1 15.8 %all-to-all-start.4 = ((bf16[16,96,128]{2,1,0:T(8,128)(2,1)}), bf16[16,96,128]{2,1,0:T(8,128)(2,1)S(1)}, u32[]{:S(2)}, u32[]{:S(2)}) async-start(bf16[16,96,128]{2,1,0:T(8,128)(2,1)} %bitcast.45), calls=%async_computation.4 | async-start | bytes 786432 | tf_op jit(solution)/shard_map/all_to_all | solution.py:153
  164.5 18.1 %collective-permute-start.15 = (bf16[96,256]{0,1:T(8,128)(2,1)S(1)}, bf16[96,256]{0,1:T(8,128)(2,1)S(1)}, u32[]{:S(2)}, u32[]{:S(2)}) collective-permute-start(bf16[96,256]{0,1:T(8,128)(2,1)S(1)} %bitcast.102), channel_id=1, source_target_pairs={{0,256},{256,0},{1,257},{257,1},{2,258},{258,2},{3,259},{259,3},{4... | collective-permute-start | bytes 147464 | tf_op jit(solution)/shard_map/ppermute | solution.py:156

commit v3 on v2

--- a/solution.py
+++ b/solution.py
@@ -10,7 +10,6 @@
 CAP = 64
 AXES = ("zh", "y", "x", "z", "c")
 ORDER = (0, 4, 2, 1, 5, 3, 6, 7)
-PARTS = (3, 5)
 
 
 def shift(n, d):
@@ -29,23 +28,25 @@
     return lax.optimization_barrier(arrays)
 
 
-def gather_z(v):
+def gather_z(v, first):
     over = lambda a, step: lax.ppermute(a, "z", flip(8, step))
     core = lambda a: lax.ppermute(a, "c", flip(2, 1))
-    rows = v.shape[0]
-    b4, b2 = over(v, 4), over(v, 2)
+    b4, b2, b1 = over(v, 4), over(v, 2), over(v, 1)
     early = jnp.concatenate([v, b4, b2])
-    b6, b153 = over(b4, 2), over(early, 1)
-    early_other = core(early)
-    late = jnp.concatenate([b153, b6, over(b6, 1)])
+    b6, b53 = over(b4, 2), over(early[v.shape[0] :], 1)
+    b153 = jnp.concatenate([b1, b53])
+    late = [b153, b6, over(b6, 1)]
+    if first == len(ORDER):
+        rows = [jnp.concatenate([early] + late)]
+        return rows[0], core(rows[0])
+    late, early_other = held(jnp.concatenate(late), core(early))
     return early, early_other, late, core(late)
 
 
-def block_order():
+def block_order(first):
     z, c = lax.axis_index("z"), lax.axis_index("c")
-    first = [(i, j) for j in (0, 1) for i in ORDER[: PARTS[0]]]
-    last = [(i, j) for j in (0, 1) for i in ORDER[PARTS[0] :]]
-    return jnp.stack([(z ^ i) * 2 + (c ^ j) for i, j in first + last]).astype(jnp.int32)
+    blocks = [(i, j) for some in (ORDER[:first], ORDER[first:]) for j in (0, 1) for i in some]
+    return jnp.stack([(z ^ i) * 2 + (c ^ j) for i, j in blocks]).astype(jnp.int32)
 
 
 def ordered(order, operands, body, blocks, out_block, out_shape):
@@ -121,7 +122,6 @@
 def local(tokens, expert_ids, routing_weights, gate_weight, up_weight, down_weight):
     zh = lax.axis_index("zh")
     feats, lanes = tokens.shape[1], 2 * CAP
-    order = block_order()
 
     targets = route(expert_ids)
     slot = lax.broadcasted_iota(jnp.int32, (4 * CAP, tokens.shape[0]), 0)
@@ -132,14 +132,14 @@
     packed = [contract(tokens, (a | b).astype(BF), 0, 1).astype(BF) for a, b in hits]
     _, gate_weight, up_weight = held(packed[1][:8], gate_weight, up_weight)
     packed[1] = lax.ppermute(packed[1], "zh", flip(2, 1))
-    gate_up = ordered_gate_up(order, gate_weight[0], up_weight[0])
+    gate_up = ordered_gate_up(block_order(8), gate_weight[0], up_weight[0])
 
     v = jnp.concatenate([p.reshape(feats, 4, CAP) for p in packed], axis=2).transpose(1, 0, 2)
     v = lax.all_to_all(v, "y", 0, 0).transpose(1, 0, 2).reshape(feats, -1)
     _, gate_up, down_weight = held(v[:8, :128], gate_up, down_weight)
     gate_up = lax.all_to_all(gate_up, "x", 0, 0)
-    down = ordered_down(order, down_weight[0].T)
-    parts = gather_z(v)
+    down = ordered_down(block_order(3), down_weight[0].T)
+    parts = gather_z(v, 8)
     terms = times_parts(gate_up, 1, parts).astype(BF)
     both = jnp.sum(lax.all_to_all(terms, "x", 0, 0).astype(F32), axis=0)
     gate, up = both[:128], both[128:]
@@ -147,7 +147,7 @@
 
     hidden, down = held(hidden, down)
     down = lax.all_to_all(down, "x", 0, 0)
-    parts = gather_z(hidden)
+    parts = gather_z(hidden, 3)
     terms = times_parts(down, 2, parts).astype(BF)
     terms = terms.reshape(4, feats, 4, lanes).transpose(2, 0, 1, 3).reshape(16, feats, lanes)
     terms = lax.all_to_all(terms, ("y", "x"), 0, 0).reshape(4, 4, feats, lanes)

time: 185 us -> 181 us (0.978)
  the two profiles are of different devices: /device:TPU:32 before, /device:TPU:96 now
where the time goes in v3:
time: 181 us; the launch traced here: 180 us
  starting transfers between devices  95 us (52%)
  waiting for transfers between devices  62.3 us (34%)
  local copies, waits for them, and re-layouts  9.61 us (5%)
  matrix products  7.81 us (4%)
  Pallas kernels  3.75 us (2%)
    ppermute x12, starting transfers between devices, gather_z(): over = lambda a, step: lax.ppermute(a, 'z', flip(8, step))  42.5 us
    ppermute x12, waiting for transfers between devices, gather_z(): over = lambda a, step: lax.ppermute(a, 'z', flip(8, step))  26.5 us
    ppermute x1, starting transfers between devices, local(): packed[1] = lax.ppermute(packed[1], 'zh', flip(2, 1))  13 us
    all_to_all x1, waiting for transfers between devices, local(): both = jnp.sum(lax.all_to_all(terms, 'x', 0, 0).astype(F32), axis=0)  12.7 us
    all_to_all x1, waiting for transfers between devices, local(): terms = lax.all_to_all(terms, ('y', 'x'), 0, 0).reshape(4, 4, feats, lanes)  10.4 us
    ppermute x1, starting transfers between devices, local(): backs[1] = lax.ppermute(backs[1], 'zh', flip(2, 1))  10.1 us
    dot_general x13, matrix products, contract(): lax.dot_general(a, b, (((da,), (db,)), ((), ())), preferred_element_type=...  7.81 us
    all_to_all x1, starting transfers between devices, local(): terms = lax.all_to_all(terms, ('y', 'x'), 0, 0).reshape(4, 4, feats, lanes)  6.45 us
  transfers between devices with their start and end apart: 22, of which 14 were waited for; matrix products, arithmetic and copies ran while one was open for 2% of the time, Pallas kernels for 2%

profile of v3, /device:TPU:96, one launch (start us, length us, event | category | flops | bytes accessed | tf_op | source)
XLA Modules:
  0.0 180.2 jit_solution(6784415058249809330)
XLA Ops:
  1.9 13.0 %collective-permute-start = (bf16[96,256]{1,0:T(8,128)(2,1)S(1)}, bf16[96,256]{1,0:T(8,128)(2,1)S(1)}, u32[]{:S(2)}, u32[]{:S(2)}) collective-permute-start(bf16[96,256]{1,0:T(8,128)(2,1)S(1)} %fusion.12), channel_id=1, source_target_pairs={{0,256},{256,0},{1,257},{257,1},{2,258},{258,2},{3,259},{259,3},{4... | collective-permute-start | bytes 147464 | tf_op jit(solution)/shard_map/ppermute | solution.py:134
  15.3 3.1 %collective-permute-done = bf16[96,256]{1,0:T(8,128)(2,1)S(1)} collective-permute-done((bf16[96,256]{1,0:T(8,128)(2,1)S(1)}, bf16[96,256]{1,0:T(8,128)(2,1)S(1)}, u32[]{:S(2)}, u32[]{:S(2)}) %collective-permute-start) | collective-permute-done | bytes 49184 | tf_op jit(solution)/shard_map/ppermute | solution.py:134
  19.3 4.5 %all-to-all-start.1 = ((bf16[4,96,128]{2,1,0:T(8,128)(2,1)}), bf16[4,96,128]{2,1,0:T(8,128)(2,1)S(1)}, u32[]{:S(2)}, u32[]{:S(2)}) async-start(bf16[4,96,128]{2,1,0:T(8,128)(2,1)} %copy.16), calls=%async_computation.1 | async-start | bytes 196608 | tf_op jit(solution)/shard_map/all_to_all | solution.py:138
  27.9 2.8 %copy.13 = bf16[4,1536,256]{1,2,0:T(8,128)(2,1)} copy(bf16[4,1536,256]{2,1,0:T(8,128)(2,1)S(1)} %bitcast.88) | data formatting | bytes 6291456 | tf_op jit(solution)/shard_map/optimization_barrier | solution.py:28
  30.7 4.3 %all-to-all-start = ((bf16[4,1536,256]{1,2,0:T(8,128)(2,1)}), bf16[4,1536,256]{1,2,0:T(8,128)(2,1)S(1)}, u32[]{:S(2)}, u32[]{:S(2)}) async-start(bf16[4,1536,256]{1,2,0:T(8,128)(2,1)} %copy.13), calls=%async_computation | async-start | bytes 6291456 | tf_op jit(solution)/shard_map/all_to_all | solution.py:140
  35.0 7.3 %collective-permute-start.1 = (bf16[96,512]{1,0:T(8,128)(2,1)S(1)}, bf16[96,512]{1,0:T(8,128)(2,1)S(1)}, u32[]{:S(2)}, u32[]{:S(2)}) collective-permute-start(bf16[96,512]{1,0:T(8,128)(2,1)S(1)} %copy_bitcast_fusion.1), channel_id=1, source_target_pairs={{0,8},{2,10},{4,12},{6,14},{8,0},{10,2},{12,4},{14,6},{1,9},{3,11}... | collective-permute-start | bytes 294920 | tf_op jit(solution)/shard_map/ppermute | solution.py:32
  44.3 3.9 %collective-permute-start.3 = (bf16[96,512]{1,0:T(8,128)(2,1)S(1)}, bf16[96,512]{1,0:T(8,128)(2,1)S(1)}, u32[]{:S(2)}, u32[]{:S(2)}) collective-permute-start(bf16[96,512]{1,0:T(8,128)(2,1)S(1)} %copy_bitcast_fusion.1), channel_id=1, source_target_pairs={{0,2},{2,0},{4,6},{6,4},{8,10},{10,8},{12,14},{14,12},{1,3},{3,1},... | collective-permute-start | bytes 294920 | tf_op jit(solution)/shard_map/ppermute | solution.py:32
  48.2 2.4 %collective-permute-done.2 = bf16[96,512]{1,0:T(8,128)(2,1)S(1)} collective-permute-done((bf16[96,512]{1,0:T(8,128)(2,1)S(1)}, bf16[96,512]{1,0:T(8,128)(2,1)S(1)}, u32[]{:S(2)}, u32[]{:S(2)}) %collective-permute-start.2) | collective-permute-done | bytes 98336 | tf_op jit(solution)/shard_map/ppermute | solution.py:32
  50.6 4.1 %collective-permute-start.4 = (bf16[192,512]{1,0:T(8,128)(2,1)S(1)}, bf16[192,512]{1,0:T(8,128)(2,1)S(1)}, u32[]{:S(2)}, u32[]{:S(2)}) collective-permute-start(bf16[192,512]{1,0:T(8,128)(2,1)S(1)} %pad_maximum_fusion.2), channel_id=1, source_target_pairs={{0,2},{2,0},{4,6},{6,4},{8,10},{10,8},{12,14},{14,12},{1,3},{3,1},... | collective-permute-start | bytes 589832 | tf_op jit(solution)/shard_map/ppermute | solution.py:32
  54.7 2.4 %collective-permute-start.5 = (bf16[96,512]{1,0:T(8,128)(2,1)S(1)}, bf16[96,512]{1,0:T(8,128)(2,1)S(1)}, u32[]{:S(2)}, u32[]{:S(2)}) collective-permute-start(bf16[96,512]{1,0:T(8,128)(2,1)S(1)} %collective-permute-done.1), channel_id=1, source_target_pairs={{0,4},{2,6},{4,0},{6,2},{8,12},{10,14},{12,8},{14,10},{1,5},{3,7},... | collective-permute-start | bytes 294920 | tf_op jit(solution)/shard_map/ppermute | solution.py:32
  57.2 5.4 %collective-permute-done.5 = bf16[96,512]{1,0:T(8,128)(2,1)S(1)} collective-permute-done((bf16[96,512]{1,0:T(8,128)(2,1)S(1)}, bf16[96,512]{1,0:T(8,128)(2,1)S(1)}, u32[]{:S(2)}, u32[]{:S(2)}) %collective-permute-start.5) | collective-permute-done | bytes 98336 | tf_op jit(solution)/shard_map/ppermute | solution.py:32
  64.6 4.5 %collective-permute-done.6 = bf16[96,512]{1,0:T(8,128)(2,1)S(1)} collective-permute-done((bf16[96,512]{1,0:T(8,128)(2,1)S(1)}, bf16[96,512]{1,0:T(8,128)(2,1)S(1)}, u32[]{:S(2)}, u32[]{:S(2)}) %collective-permute-start.6) | collective-permute-done | bytes 98336 | tf_op jit(solution)/shard_map/ppermute | solution.py:32
  71.1 2.4 %collective-permute-done.7 = bf16[768,512]{1,0:T(8,128)(2,1)} collective-permute-done((bf16[768,512]{1,0:T(8,128)(2,1)S(1)}, bf16[768,512]{1,0:T(8,128)(2,1)}, u32[]{:S(2)}, u32[]{:S(2)}) %collective-permute-start.7) | collective-permute-done | bytes 786464 | tf_op jit(solution)/shard_map/ppermute | solution.py:33
  73.5 2.2 %fusion = f32[4,256,512]{2,1,0:T(8,128)S(1)} fusion(bf16[4,1536,256]{1,2,0:T(8,128)(2,1)S(1)} %all-to-all-done, bf16[768,512]{1,0:T(8,128)(2,1)} %collective-permute-done.7), kind=kOutput, calls=%fused_computation.2 | convolution fusion | flops 805306368 | bytes 4456448 | tf_op jit(solution)/shard_map/dot_general | solution.py:24
  77.6 4.7 %all-to-all-start.2 = ((bf16[4,256,512]{2,1,0:T(8,128)(2,1)}), bf16[4,256,512]{2,1,0:T(8,128)(2,1)S(1)}, u32[]{:S(2)}, u32[]{:S(2)}) async-start(bf16[4,256,512]{2,1,0:T(8,128)(2,1)} %add_convert_fusion), calls=%async_computation.2 | async-start | bytes 2097152 | tf_op jit(solution)/shard_map/all_to_all | solution.py:144
  82.5 2.6 %shard_map.65 = bf16[4,96,2048]{2,1,0:T(8,128)(2,1)} custom-call(s32[16]{0:T(128)S(1)} %stack.87.order_ref, bf16[96,8192]{1,0:T(8,128)(2,1)S(1)} %bitcast.91), custom_call_target="tpu_custom_call" | custom-call | bytes 3145728 | tf_op jit(solution)/shard_map/pallas_call | solution.py:53
  85.0 12.7 %all-to-all-done.2 = bf16[4,256,512]{2,1,0:T(8,128)(2,1)S(1)} async-done(((bf16[4,256,512]{2,1,0:T(8,128)(2,1)}), bf16[4,256,512]{2,1,0:T(8,128)(2,1)S(1)}, u32[]{:S(2)}, u32[]{:S(2)}) %all-to-all-start.2) | async-done | bytes 1048608 | tf_op jit(solution)/shard_map/all_to_all | solution.py:144
  98.0 5.8 %collective-permute-start.8 = (bf16[128,512]{1,0:T(8,128)(2,1)S(1)}, bf16[128,512]{1,0:T(8,128)(2,1)S(1)}, u32[]{:S(2)}, u32[]{:S(2)}) collective-permute-start(bf16[128,512]{1,0:T(8,128)(2,1)S(1)} %fusion.26), channel_id=1, source_target_pairs={{0,8},{2,10},{4,12},{6,14},{8,0},{10,2},{12,4},{14,6},{1,9},{3,11}... | collective-permute-start | bytes 393224 | tf_op jit(solution)/shard_map/ppermute | solution.py:32
  103.8 2.2 %collective-permute-start.9 = (bf16[128,512]{1,0:T(8,128)(2,1)S(1)}, bf16[128,512]{1,0:T(8,128)(2,1)S(1)}, u32[]{:S(2)}, u32[]{:S(2)}) collective-permute-start(bf16[128,512]{1,0:T(8,128)(2,1)S(1)} %fusion.26), channel_id=1, source_target_pairs={{0,4},{2,6},{4,0},{6,2},{8,12},{10,14},{12,8},{14,10},{1,5},{3,7},... | collective-permute-start | bytes 393224 | tf_op jit(solution)/shard_map/ppermute | solution.py:32
  106.0 3.6 %all-to-all-start.3 = ((bf16[4,96,2048]{2,1,0:T(8,128)(2,1)}), bf16[4,96,2048]{2,1,0:T(8,128)(2,1)S(1)}, u32[]{:S(2)}, u32[]{:S(2)}) async-start(bf16[4,96,2048]{2,1,0:T(8,128)(2,1)} %shard_map.65), calls=%async_computation.3 | async-start | bytes 3145728 | tf_op jit(solution)/shard_map/all_to_all | solution.py:149
  109.6 2.9 %collective-permute-done.8 = bf16[128,512]{1,0:T(8,128)(2,1)S(1)} collective-permute-done((bf16[128,512]{1,0:T(8,128)(2,1)S(1)}, bf16[128,512]{1,0:T(8,128)(2,1)S(1)}, u32[]{:S(2)}, u32[]{:S(2)}) %collective-permute-start.8) | collective-permute-done | bytes 131104 | tf_op jit(solution)/shard_map/ppermute | solution.py:32
  112.5 2.0 %collective-permute-done.9 = bf16[128,512]{1,0:T(8,128)(2,1)S(1)} collective-permute-done((bf16[128,512]{1,0:T(8,128)(2,1)S(1)}, bf16[128,512]{1,0:T(8,128)(2,1)S(1)}, u32[]{:S(2)}, u32[]{:S(2)}) %collective-permute-start.9) | collective-permute-done | bytes 131104 | tf_op jit(solution)/shard_map/ppermute | solution.py:32
  116.5 4.6 %collective-permute-start.12 = (bf16[128,512]{1,0:T(8,128)(2,1)S(1)}, bf16[128,512]{1,0:T(8,128)(2,1)S(1)}, u32[]{:S(2)}, u32[]{:S(2)}) collective-permute-start(bf16[128,512]{1,0:T(8,128)(2,1)S(1)} %collective-permute-done.8), channel_id=1, source_target_pairs={{0,4},{2,6},{4,0},{6,2},{8,12},{10,14},{12,8},{14,10},{1,5},{3,7},... | collective-permute-start | bytes 393224 | tf_op jit(solution)/shard_map/ppermute | solution.py:32
  121.1 3.4 %collective-permute-start.11 = (bf16[256,512]{1,0:T(8,128)(2,1)S(1)}, bf16[256,512]{1,0:T(8,128)(2,1)S(1)}, u32[]{:S(2)}, u32[]{:S(2)}) collective-permute-start(bf16[256,512]{1,0:T(8,128)(2,1)S(1)} %pad_maximum_fusion.1), channel_id=1, source_target_pairs={{0,2},{2,0},{4,6},{6,4},{8,10},{10,8},{12,14},{14,12},{1,3},{3,1},... | collective-permute-start | bytes 786440 | tf_op jit(solution)/shard_map/ppermute | solution.py:32
  124.5 2.4 %collective-permute-start.10 = (bf16[128,512]{1,0:T(8,128)(2,1)S(1)}, bf16[128,512]{1,0:T(8,128)(2,1)S(1)}, u32[]{:S(2)}, u32[]{:S(2)}) collective-permute-start(bf16[128,512]{1,0:T(8,128)(2,1)S(1)} %fusion.26), channel_id=1, source_target_pairs={{0,2},{2,0},{4,6},{6,4},{8,10},{10,8},{12,14},{14,12},{1,3},{3,1},... | collective-permute-start | bytes 393224 | tf_op jit(solution)/shard_map/ppermute | solution.py:32
  128.1 2.6 %collective-permute-start.13 = (bf16[128,512]{1,0:T(8,128)(2,1)S(1)}, bf16[128,512]{1,0:T(8,128)(2,1)S(1)}, u32[]{:S(2)}, u32[]{:S(2)}) collective-permute-start(bf16[128,512]{1,0:T(8,128)(2,1)S(1)} %collective-permute-done.12), channel_id=1, source_target_pairs={{0,2},{2,0},{4,6},{6,4},{8,10},{10,8},{12,14},{14,12},{1,3},{3,1},... | collective-permute-start | bytes 393224 | tf_op jit(solution)/shard_map/ppermute | solution.py:32
  130.7 5.8 %collective-permute-done.10 = bf16[128,512]{1,0:T(8,128)(2,1)S(1)} collective-permute-done((bf16[128,512]{1,0:T(8,128)(2,1)S(1)}, bf16[128,512]{1,0:T(8,128)(2,1)S(1)}, u32[]{:S(2)}, u32[]{:S(2)}) %collective-permute-start.10) | collective-permute-done | bytes 131104 | tf_op jit(solution)/shard_map/ppermute | solution.py:32
  136.5 2.3 %collective-permute-done.13 = bf16[128,512]{1,0:T(8,128)(2,1)S(1)} collective-permute-done((bf16[128,512]{1,0:T(8,128)(2,1)S(1)}, bf16[128,512]{1,0:T(8,128)(2,1)S(1)}, u32[]{:S(2)}, u32[]{:S(2)}) %collective-permute-start.13) | collective-permute-done | bytes 131104 | tf_op jit(solution)/shard_map/ppermute | solution.py:32
  145.7 6.5 %all-to-all-start.4 = ((bf16[16,96,128]{2,1,0:T(8,128)(2,1)}), bf16[16,96,128]{2,1,0:T(8,128)(2,1)S(1)}, u32[]{:S(2)}, u32[]{:S(2)}) async-start(bf16[16,96,128]{2,1,0:T(8,128)(2,1)} %bitcast.43), calls=%async_computation.4 | async-start | bytes 786432 | tf_op jit(solution)/shard_map/all_to_all | solution.py:153
  152.2 10.4 %all-to-all-done.4 = bf16[16,96,128]{2,1,0:T(8,128)(2,1)S(1)} async-done(((bf16[16,96,128]{2,1,0:T(8,128)(2,1)}), bf16[16,96,128]{2,1,0:T(8,128)(2,1)S(1)}, u32[]{:S(2)}, u32[]{:S(2)}) %all-to-all-start.4) | async-done | bytes 393248 | tf_op jit(solution)/shard_map/all_to_all | solution.py:153
  163.1 10.1 %collective-permute-start.16 = (bf16[96,256]{0,1:T(8,128)(2,1)S(1)}, bf16[96,256]{0,1:T(8,128)(2,1)S(1)}, u32[]{:S(2)}, u32[]{:S(2)}) collective-permute-start(bf16[96,256]{0,1:T(8,128)(2,1)S(1)} %bitcast.97), channel_id=1, source_target_pairs={{0,256},{256,0},{1,257},{257,1},{2,258},{258,2},{3,259},{259,3},{4... | collective-permute-start | bytes 147464 | tf_op jit(solution)/shard_map/ppermute | solution.py:156
  173.5 5.6 %collective-permute-done.16 = bf16[96,256]{0,1:T(8,128)(2,1)S(1)} collective-permute-done((bf16[96,256]{0,1:T(8,128)(2,1)S(1)}, bf16[96,256]{0,1:T(8,128)(2,1)S(1)}, u32[]{:S(2)}, u32[]{:S(2)}) %collective-permute-start.16) | collective-permute-done | bytes 49184 | tf_op jit(solution)/shard_map/ppermute | solution.py:156
  (79 shorter events, 27.1 us)
Async XLA Ops:
  0.0 1.7 copy-start
  1.9 16.5 %collective-permute-start = (bf16[96,256]{1,0:T(8,128)(2,1)S(1)}, bf16[96,256]{1,0:T(8,128)(2,1)S(1)}, u32[]{:S(2)}, u32[]{:S(2)}) collective-permute-start(bf16[96,256]{1,0:T(8,128)(2,1)S(1)} %fusion.12), channel_id=1, source_target_pairs={{0,256},{256,0},{1,257},{257,1},{2,258},{258,2},{3,259},{259,3},{4... | collective-permute-start | bytes 147464 | tf_op jit(solution)/shard_map/ppermute | solution.py:134
  19.3 11.4 %all-to-all-start.1 = ((bf16[4,96,128]{2,1,0:T(8,128)(2,1)}), bf16[4,96,128]{2,1,0:T(8,128)(2,1)S(1)}, u32[]{:S(2)}, u32[]{:S(2)}) async-start(bf16[4,96,128]{2,1,0:T(8,128)(2,1)} %copy.16), calls=%async_computation.1 | async-start | bytes 196608 | tf_op jit(solution)/shard_map/all_to_all | solution.py:138
  23.9 1.4 copy-start.1
  25.3 1.4 copy-start.2
  30.7 42.7 %all-to-all-start = ((bf16[4,1536,256]{1,2,0:T(8,128)(2,1)}), bf16[4,1536,256]{1,2,0:T(8,128)(2,1)S(1)}, u32[]{:S(2)}, u32[]{:S(2)}) async-start(bf16[4,1536,256]{1,2,0:T(8,128)(2,1)} %copy.13), calls=%async_computation | async-start | bytes 6291456 | tf_op jit(solution)/shard_map/all_to_all | solution.py:140
  35.0 13.2 %collective-permute-start.1 = (bf16[96,512]{1,0:T(8,128)(2,1)S(1)}, bf16[96,512]{1,0:T(8,128)(2,1)S(1)}, u32[]{:S(2)}, u32[]{:S(2)}) collective-permute-start(bf16[96,512]{1,0:T(8,128)(2,1)S(1)} %copy_bitcast_fusion.1), channel_id=1, source_target_pairs={{0,8},{2,10},{4,12},{6,14},{8,0},{10,2},{12,4},{14,6},{1,9},{3,11}... | collective-permute-start | bytes 294920 | tf_op jit(solution)/shard_map/ppermute | solution.py:32
  42.4 8.2 %collective-permute-start.2 = (bf16[96,512]{1,0:T(8,128)(2,1)S(1)}, bf16[96,512]{1,0:T(8,128)(2,1)S(1)}, u32[]{:S(2)}, u32[]{:S(2)}) collective-permute-start(bf16[96,512]{1,0:T(8,128)(2,1)S(1)} %copy_bitcast_fusion.1), channel_id=1, source_target_pairs={{0,4},{2,6},{4,0},{6,2},{8,12},{10,14},{12,8},{14,10},{1,5},{3,7},... | collective-permute-start | bytes 294920 | tf_op jit(solution)/shard_map/ppermute | solution.py:32
  44.3 12.9 %collective-permute-start.3 = (bf16[96,512]{1,0:T(8,128)(2,1)S(1)}, bf16[96,512]{1,0:T(8,128)(2,1)S(1)}, u32[]{:S(2)}, u32[]{:S(2)}) collective-permute-start(bf16[96,512]{1,0:T(8,128)(2,1)S(1)} %copy_bitcast_fusion.1), channel_id=1, source_target_pairs={{0,2},{2,0},{4,6},{6,4},{8,10},{10,8},{12,14},{14,12},{1,3},{3,1},... | collective-permute-start | bytes 294920 | tf_op jit(solution)/shard_map/ppermute | solution.py:32
  50.6 13.9 %collective-permute-start.4 = (bf16[192,512]{1,0:T(8,128)(2,1)S(1)}, bf16[192,512]{1,0:T(8,128)(2,1)S(1)}, u32[]{:S(2)}, u32[]{:S(2)}) collective-permute-start(bf16[192,512]{1,0:T(8,128)(2,1)S(1)} %pad_maximum_fusion.2), channel_id=1, source_target_pairs={{0,2},{2,0},{4,6},{6,4},{8,10},{10,8},{12,14},{14,12},{1,3},{3,1},... | collective-permute-start | bytes 589832 | tf_op jit(solution)/shard_map/ppermute | solution.py:32
  54.7 7.9 %collective-permute-start.5 = (bf16[96,512]{1,0:T(8,128)(2,1)S(1)}, bf16[96,512]{1,0:T(8,128)(2,1)S(1)}, u32[]{:S(2)}, u32[]{:S(2)}) collective-permute-start(bf16[96,512]{1,0:T(8,128)(2,1)S(1)} %collective-permute-done.1), channel_id=1, source_target_pairs={{0,4},{2,6},{4,0},{6,2},{8,12},{10,14},{12,8},{14,10},{1,5},{3,7},... | collective-permute-start | bytes 294920 | tf_op jit(solution)/shard_map/ppermute | solution.py:32
  62.6 6.5 %collective-permute-start.6 = (bf16[96,512]{1,0:T(8,128)(2,1)S(1)}, bf16[96,512]{1,0:T(8,128)(2,1)S(1)}, u32[]{:S(2)}, u32[]{:S(2)}) collective-permute-start(bf16[96,512]{1,0:T(8,128)(2,1)S(1)} %collective-permute-done.5), channel_id=1, source_target_pairs={{0,2},{2,0},{4,6},{6,4},{8,10},{10,8},{12,14},{14,12},{1,3},{3,1},... | collective-permute-start | bytes 294920 | tf_op jit(solution)/shard_map/ppermute | solution.py:32
  69.1 1.9 %copy-start.6 = (bf16[768,512]{1,0:T(8,128)(2,1)}, bf16[768,512]{1,0:T(8,128)(2,1)S(1)}, u32[]{:S(2)}) copy-start(bf16[768,512]{1,0:T(8,128)(2,1)S(1)} %constant_dynamic-update-slice_fusion) | copy-start | bytes 2359300
  69.1 4.3 %collective-permute-start.7 = (bf16[768,512]{1,0:T(8,128)(2,1)S(1)}, bf16[768,512]{1,0:T(8,128)(2,1)}, u32[]{:S(2)}, u32[]{:S(2)}) collective-permute-start(bf16[768,512]{1,0:T(8,128)(2,1)S(1)} %constant_dynamic-update-slice_fusion), channel_id=1, source_target_pairs={{0,1},{1,0},{2,3},{3,2},{4,5},{5,4},{6,7},{7,6},{8,9},{9,8},{10,11... | collective-permute-start | bytes 2359304 | tf_op jit(solution)/shard_map/ppermute | solution.py:33
  73.5 2.2 %copy-start.7 = (bf16[768,512]{1,0:T(8,128)(2,1)S(1)}, bf16[768,512]{1,0:T(8,128)(2,1)}, u32[]{:S(2)}) copy-start(bf16[768,512]{1,0:T(8,128)(2,1)} %copy-done.6) | copy-start | bytes 2359300
  77.6 4.8 %copy-start.3 = (bf16[1,8192,96]{1,2,0:T(8,128)(2,1)S(1)}, bf16[1,8192,96]{1,2,0:T(8,128)(2,1)}, u32[]{:S(2)}) copy-start(bf16[1,8192,96]{1,2,0:T(8,128)(2,1)} %param.11) | copy-start | bytes 4718596
  77.6 20.1 %all-to-all-start.2 = ((bf16[4,256,512]{2,1,0:T(8,128)(2,1)}), bf16[4,256,512]{2,1,0:T(8,128)(2,1)S(1)}, u32[]{:S(2)}, u32[]{:S(2)}) async-start(bf16[4,256,512]{2,1,0:T(8,128)(2,1)} %add_convert_fusion), calls=%async_computation.2 | async-start | bytes 2097152 | tf_op jit(solution)/shard_map/all_to_all | solution.py:144
  98.0 14.5 %collective-permute-start.8 = (bf16[128,512]{1,0:T(8,128)(2,1)S(1)}, bf16[128,512]{1,0:T(8,128)(2,1)S(1)}, u32[]{:S(2)}, u32[]{:S(2)}) collective-permute-start(bf16[128,512]{1,0:T(8,128)(2,1)S(1)} %fusion.26), channel_id=1, source_target_pairs={{0,8},{2,10},{4,12},{6,14},{8,0},{10,2},{12,4},{14,6},{1,9},{3,11}... | collective-permute-start | bytes 393224 | tf_op jit(solution)/shard_map/ppermute | solution.py:32
  103.8 10.8 %collective-permute-start.9 = (bf16[128,512]{1,0:T(8,128)(2,1)S(1)}, bf16[128,512]{1,0:T(8,128)(2,1)S(1)}, u32[]{:S(2)}, u32[]{:S(2)}) collective-permute-start(bf16[128,512]{1,0:T(8,128)(2,1)S(1)} %fusion.26), channel_id=1, source_target_pairs={{0,4},{2,6},{4,0},{6,2},{8,12},{10,14},{12,8},{14,10},{1,5},{3,7},... | collective-permute-start | bytes 393224 | tf_op jit(solution)/shard_map/ppermute | solution.py:32
  106.0 35.5 %all-to-all-start.3 = ((bf16[4,96,2048]{2,1,0:T(8,128)(2,1)}), bf16[4,96,2048]{2,1,0:T(8,128)(2,1)S(1)}, u32[]{:S(2)}, u32[]{:S(2)}) async-start(bf16[4,96,2048]{2,1,0:T(8,128)(2,1)} %shard_map.65), calls=%async_computation.3 | async-start | bytes 3145728 | tf_op jit(solution)/shard_map/all_to_all | solution.py:149
  114.6 24.3 %collective-permute-start.14 = (bf16[384,512]{1,0:T(8,128)(2,1)S(1)}, bf16[384,512]{1,0:T(8,128)(2,1)S(1)}, u32[]{:S(2)}, u32[]{:S(2)}) collective-permute-start(bf16[384,512]{1,0:T(8,128)(2,1)S(1)} %constant_dynamic-update-slice_fusion.7), channel_id=1, source_target_pairs={{0,1},{1,0},{2,3},{3,2},{4,5},{5,4},{6,7},{7,6},{8,9},{9,8},{10,11... | collective-permute-start | bytes 1179656 | tf_op jit(solution)/shard_map/ppermute | solution.py:33
  116.5 11.6 %collective-permute-start.12 = (bf16[128,512]{1,0:T(8,128)(2,1)S(1)}, bf16[128,512]{1,0:T(8,128)(2,1)S(1)}, u32[]{:S(2)}, u32[]{:S(2)}) collective-permute-start(bf16[128,512]{1,0:T(8,128)(2,1)S(1)} %collective-permute-done.8), channel_id=1, source_target_pairs={{0,4},{2,6},{4,0},{6,2},{8,12},{10,14},{12,8},{14,10},{1,5},{3,7},... | collective-permute-start | bytes 393224 | tf_op jit(solution)/shard_map/ppermute | solution.py:32
  121.1 17.7 %collective-permute-start.11 = (bf16[256,512]{1,0:T(8,128)(2,1)S(1)}, bf16[256,512]{1,0:T(8,128)(2,1)S(1)}, u32[]{:S(2)}, u32[]{:S(2)}) collective-permute-start(bf16[256,512]{1,0:T(8,128)(2,1)S(1)} %pad_maximum_fusion.1), channel_id=1, source_target_pairs={{0,2},{2,0},{4,6},{6,4},{8,10},{10,8},{12,14},{14,12},{1,3},{3,1},... | collective-permute-start | bytes 786440 | tf_op jit(solution)/shard_map/ppermute | solution.py:32
  124.5 12.0 %collective-permute-start.10 = (bf16[128,512]{1,0:T(8,128)(2,1)S(1)}, bf16[128,512]{1,0:T(8,128)(2,1)S(1)}, u32[]{:S(2)}, u32[]{:S(2)}) collective-permute-start(bf16[128,512]{1,0:T(8,128)(2,1)S(1)} %fusion.26), channel_id=1, source_target_pairs={{0,2},{2,0},{4,6},{6,4},{8,10},{10,8},{12,14},{14,12},{1,3},{3,1},... | collective-permute-start | bytes 393224 | tf_op jit(solution)/shard_map/ppermute | solution.py:32
  128.1 10.7 %collective-permute-start.13 = (bf16[128,512]{1,0:T(8,128)(2,1)S(1)}, bf16[128,512]{1,0:T(8,128)(2,1)S(1)}, u32[]{:S(2)}, u32[]{:S(2)}) collective-permute-start(bf16[128,512]{1,0:T(8,128)(2,1)S(1)} %collective-permute-done.12), channel_id=1, source_target_pairs={{0,2},{2,0},{4,6},{6,4},{8,10},{10,8},{12,14},{14,12},{1,3},{3,1},... | collective-permute-start | bytes 393224 | tf_op jit(solution)/shard_map/ppermute | solution.py:32
  138.9 0.8 copy-start.4
  139.6 4.0 %collective-permute-start.15 = (bf16[640,512]{1,0:T(8,128)(2,1)S(1)}, bf16[640,512]{1,0:T(8,128)(2,1)S(1)}, u32[]{:S(2)}, u32[]{:S(2)}) collective-permute-start(bf16[640,512]{1,0:T(8,128)(2,1)S(1)} %pad_maximum_fusion), channel_id=1, source_target_pairs={{0,1},{1,0},{2,3},{3,2},{4,5},{5,4},{6,7},{7,6},{8,9},{9,8},{10,11... | collective-permute-start | bytes 1966088 | tf_op jit(solution)/shard_map/ppermute | solution.py:33
  141.6 2.5 %copy-start.5 = (bf16[384,512]{1,0:T(8,128)(2,1)S(1)}, bf16[384,512]{1,0:T(8,128)(2,1)}, u32[]{:S(2)}) copy-start(bf16[384,512]{1,0:T(8,128)(2,1)} %copy-done.4) | copy-start | bytes 1179652
  144.9 7.3 %copy-start.8 = (f32[256,2]{0,1:T(2,128)S(1)}, f32[256,2]{0,1:T(2,128)}, u32[]{:S(2)}) copy-start(f32[256,2]{0,1:T(2,128)} %param.8) | copy-start | bytes 6148
  145.7 16.8 %all-to-all-start.4 = ((bf16[16,96,128]{2,1,0:T(8,128)(2,1)}), bf16[16,96,128]{2,1,0:T(8,128)(2,1)S(1)}, u32[]{:S(2)}, u32[]{:S(2)}) async-start(bf16[16,96,128]{2,1,0:T(8,128)(2,1)} %bitcast.43), calls=%async_computation.4 | async-start | bytes 786432 | tf_op jit(solution)/shard_map/all_to_all | solution.py:153
  163.1 16.0 %collective-permute-start.16 = (bf16[96,256]{0,1:T(8,128)(2,1)S(1)}, bf16[96,256]{0,1:T(8,128)(2,1)S(1)}, u32[]{:S(2)}, u32[]{:S(2)}) collective-permute-start(bf16[96,256]{0,1:T(8,128)(2,1)S(1)} %bitcast.97), channel_id=1, source_target_pairs={{0,256},{256,0},{1,257},{257,1},{2,258},{258,2},{3,259},{259,3},{4... | collective-permute-start | bytes 147464 | tf_op jit(solution)/shard_map/ppermute | solution.py:156

commit v4 on v3

--- a/solution.py
+++ b/solution.py
@@ -138,7 +138,7 @@
     v = lax.all_to_all(v, "y", 0, 0).transpose(1, 0, 2).reshape(feats, -1)
     _, gate_up, down_weight = held(v[:8, :128], gate_up, down_weight)
     gate_up = lax.all_to_all(gate_up, "x", 0, 0)
-    down = ordered_down(block_order(3), down_weight[0].T)
+    down = ordered_down(block_order(8), down_weight[0].T)
     parts = gather_z(v, 8)
     terms = times_parts(gate_up, 1, parts).astype(BF)
     both = jnp.sum(lax.all_to_all(terms, "x", 0, 0).astype(F32), axis=0)
@@ -147,7 +147,7 @@
 
     hidden, down = held(hidden, down)
     down = lax.all_to_all(down, "x", 0, 0)
-    parts = gather_z(hidden, 3)
+    parts = gather_z(hidden, 8)
     terms = times_parts(down, 2, parts).astype(BF)
     terms = terms.reshape(4, feats, 4, lanes).transpose(2, 0, 1, 3).reshape(16, feats, lanes)
     terms = lax.all_to_all(terms, ("y", "x"), 0, 0).reshape(4, 4, feats, lanes)

time: 181 us -> 181 us (level)
  the two profiles are of different devices: /device:TPU:96 before, /device:TPU:32 now
where the time goes in v4:
time: 181 us; the launch traced here: 180 us
  starting transfers between devices  98.6 us (54%)
  waiting for transfers between devices  58.7 us (32%)
  local copies, waits for them, and re-layouts  8.79 us (5%)
  matrix products  8.49 us (5%)
  Pallas kernels  3.72 us (2%)
    ppermute x12, starting transfers between devices, gather_z(): over = lambda a, step: lax.ppermute(a, 'z', flip(8, step))  46.1 us
    ppermute x12, waiting for transfers between devices, gather_z(): over = lambda a, step: lax.ppermute(a, 'z', flip(8, step))  20.8 us
    ppermute x1, starting transfers between devices, local(): packed[1] = lax.ppermute(packed[1], 'zh', flip(2, 1))  14.8 us
    all_to_all x1, waiting for transfers between devices, local(): both = jnp.sum(lax.all_to_all(terms, 'x', 0, 0).astype(F32), axis=0)  12.9 us
    ppermute x1, starting transfers between devices, local(): backs[1] = lax.ppermute(backs[1], 'zh', flip(2, 1))  10.7 us
    all_to_all x1, waiting for transfers between devices, local(): terms = lax.all_to_all(terms, ('y', 'x'), 0, 0).reshape(4, 4, feats, lanes)  10.4 us
    dot_general x11, matrix products, contract(): lax.dot_general(a, b, (((da,), (db,)), ((), ())), preferred_element_type=...  8.49 us
    ppermute x1, waiting for transfers between devices, local(): backs[1] = lax.ppermute(backs[1], 'zh', flip(2, 1))  6.78 us
  transfers between devices with their start and end apart: 21, of which 13 were waited for; matrix products, arithmetic and copies ran while one was open for 2% of the time, Pallas kernels for 2%

profile of v4, /device:TPU:32, one launch (start us, length us, event | category | flops | bytes accessed | tf_op | source)
XLA Modules:
  0.0 180.0 jit_solution(9668457188187659499)
XLA Ops:
  1.9 14.8 %collective-permute-start = (bf16[96,256]{1,0:T(8,128)(2,1)S(1)}, bf16[96,256]{1,0:T(8,128)(2,1)S(1)}, u32[]{:S(2)}, u32[]{:S(2)}) collective-permute-start(bf16[96,256]{1,0:T(8,128)(2,1)S(1)} %fusion.10), channel_id=1, source_target_pairs={{0,256},{256,0},{1,257},{257,1},{2,258},{258,2},{3,259},{259,3},{4... | collective-permute-start | bytes 147464 | tf_op jit(solution)/shard_map/ppermute | solution.py:134
  17.1 2.8 %collective-permute-done = bf16[96,256]{1,0:T(8,128)(2,1)S(1)} collective-permute-done((bf16[96,256]{1,0:T(8,128)(2,1)S(1)}, bf16[96,256]{1,0:T(8,128)(2,1)S(1)}, u32[]{:S(2)}, u32[]{:S(2)}) %collective-permute-start) | collective-permute-done | bytes 49184 | tf_op jit(solution)/shard_map/ppermute | solution.py:134
  20.8 4.5 %all-to-all-start.1 = ((bf16[4,96,128]{2,1,0:T(8,128)(2,1)}), bf16[4,96,128]{2,1,0:T(8,128)(2,1)S(1)}, u32[]{:S(2)}, u32[]{:S(2)}) async-start(bf16[4,96,128]{2,1,0:T(8,128)(2,1)} %copy.16), calls=%async_computation.1 | async-start | bytes 196608 | tf_op jit(solution)/shard_map/all_to_all | solution.py:138
  29.4 2.9 %copy.13 = bf16[4,1536,256]{1,2,0:T(8,128)(2,1)} copy(bf16[4,1536,256]{2,1,0:T(8,128)(2,1)S(1)} %bitcast.82) | data formatting | bytes 6291456 | tf_op jit(solution)/shard_map/optimization_barrier | solution.py:28
  32.2 4.3 %all-to-all-start = ((bf16[4,1536,256]{1,2,0:T(8,128)(2,1)}), bf16[4,1536,256]{1,2,0:T(8,128)(2,1)S(1)}, u32[]{:S(2)}, u32[]{:S(2)}) async-start(bf16[4,1536,256]{1,2,0:T(8,128)(2,1)} %copy.13), calls=%async_computation | async-start | bytes 6291456 | tf_op jit(solution)/shard_map/all_to_all | solution.py:140
  36.5 5.8 %collective-permute-start.1 = (bf16[96,512]{1,0:T(8,128)(2,1)S(1)}, bf16[96,512]{1,0:T(8,128)(2,1)S(1)}, u32[]{:S(2)}, u32[]{:S(2)}) collective-permute-start(bf16[96,512]{1,0:T(8,128)(2,1)S(1)} %copy_bitcast_fusion.1), channel_id=1, source_target_pairs={{0,8},{2,10},{4,12},{6,14},{8,0},{10,2},{12,4},{14,6},{1,9},{3,11}... | collective-permute-start | bytes 294920 | tf_op jit(solution)/shard_map/ppermute | solution.py:32
  42.4 5.2 %collective-permute-start.2 = (bf16[96,512]{1,0:T(8,128)(2,1)S(1)}, bf16[96,512]{1,0:T(8,128)(2,1)S(1)}, u32[]{:S(2)}, u32[]{:S(2)}) collective-permute-start(bf16[96,512]{1,0:T(8,128)(2,1)S(1)} %copy_bitcast_fusion.1), channel_id=1, source_target_pairs={{0,4},{2,6},{4,0},{6,2},{8,12},{10,14},{12,8},{14,10},{1,5},{3,7},... | collective-permute-start | bytes 294920 | tf_op jit(solution)/shard_map/ppermute | solution.py:32
  47.6 3.9 %collective-permute-start.3 = (bf16[96,512]{1,0:T(8,128)(2,1)S(1)}, bf16[96,512]{1,0:T(8,128)(2,1)S(1)}, u32[]{:S(2)}, u32[]{:S(2)}) collective-permute-start(bf16[96,512]{1,0:T(8,128)(2,1)S(1)} %copy_bitcast_fusion.1), channel_id=1, source_target_pairs={{0,2},{2,0},{4,6},{6,4},{8,10},{10,8},{12,14},{14,12},{1,3},{3,1},... | collective-permute-start | bytes 294920 | tf_op jit(solution)/shard_map/ppermute | solution.py:32
  51.9 3.7 %collective-permute-start.4 = (bf16[192,512]{1,0:T(8,128)(2,1)S(1)}, bf16[192,512]{1,0:T(8,128)(2,1)S(1)}, u32[]{:S(2)}, u32[]{:S(2)}) collective-permute-start(bf16[192,512]{1,0:T(8,128)(2,1)S(1)} %pad_maximum_fusion.1), channel_id=1, source_target_pairs={{0,2},{2,0},{4,6},{6,4},{8,10},{10,8},{12,14},{14,12},{1,3},{3,1},... | collective-permute-start | bytes 589832 | tf_op jit(solution)/shard_map/ppermute | solution.py:32
  55.5 4.3 %collective-permute-start.5 = (bf16[96,512]{1,0:T(8,128)(2,1)S(1)}, bf16[96,512]{1,0:T(8,128)(2,1)S(1)}, u32[]{:S(2)}, u32[]{:S(2)}) collective-permute-start(bf16[96,512]{1,0:T(8,128)(2,1)S(1)} %collective-permute-done.1), channel_id=1, source_target_pairs={{0,4},{2,6},{4,0},{6,2},{8,12},{10,14},{12,8},{14,10},{1,5},{3,7},... | collective-permute-start | bytes 294920 | tf_op jit(solution)/shard_map/ppermute | solution.py:32
  60.0 3.0 %collective-permute-done.5 = bf16[96,512]{1,0:T(8,128)(2,1)S(1)} collective-permute-done((bf16[96,512]{1,0:T(8,128)(2,1)S(1)}, bf16[96,512]{1,0:T(8,128)(2,1)S(1)}, u32[]{:S(2)}, u32[]{:S(2)}) %collective-permute-start.5) | collective-permute-done | bytes 98336 | tf_op jit(solution)/shard_map/ppermute | solution.py:32
  63.0 2.2 %collective-permute-start.6 = (bf16[96,512]{1,0:T(8,128)(2,1)S(1)}, bf16[96,512]{1,0:T(8,128)(2,1)S(1)}, u32[]{:S(2)}, u32[]{:S(2)}) collective-permute-start(bf16[96,512]{1,0:T(8,128)(2,1)S(1)} %collective-permute-done.5), channel_id=1, source_target_pairs={{0,2},{2,0},{4,6},{6,4},{8,10},{10,8},{12,14},{14,12},{1,3},{3,1},... | collective-permute-start | bytes 294920 | tf_op jit(solution)/shard_map/ppermute | solution.py:32
  65.3 4.2 %collective-permute-done.6 = bf16[96,512]{1,0:T(8,128)(2,1)S(1)} collective-permute-done((bf16[96,512]{1,0:T(8,128)(2,1)S(1)}, bf16[96,512]{1,0:T(8,128)(2,1)S(1)}, u32[]{:S(2)}, u32[]{:S(2)}) %collective-permute-start.6) | collective-permute-done | bytes 98336 | tf_op jit(solution)/shard_map/ppermute | solution.py:32
  71.4 2.4 %collective-permute-done.7 = bf16[768,512]{1,0:T(8,128)(2,1)} collective-permute-done((bf16[768,512]{1,0:T(8,128)(2,1)S(1)}, bf16[768,512]{1,0:T(8,128)(2,1)}, u32[]{:S(2)}, u32[]{:S(2)}) %collective-permute-start.7) | collective-permute-done | bytes 786464 | tf_op jit(solution)/shard_map/ppermute | solution.py:33
  73.8 2.2 %fusion = f32[4,256,512]{2,1,0:T(8,128)S(1)} fusion(bf16[4,1536,256]{1,2,0:T(8,128)(2,1)S(1)} %all-to-all-done, bf16[768,512]{1,0:T(8,128)(2,1)} %collective-permute-done.7), kind=kOutput, calls=%fused_computation.2 | convolution fusion | flops 805306368 | bytes 4456448 | tf_op jit(solution)/shard_map/dot_general | solution.py:24
  76.0 2.0 %add_convert_fusion = bf16[4,256,512]{2,1,0:T(8,128)(2,1)} fusion(f32[4,256,512]{2,1,0:T(8,128)S(1)} %fusion, bf16[4,1536,256]{1,2,0:T(8,128)(2,1)S(1)} %all-to-all-done, bf16[768,512]{1,0:T(8,128)(2,1)S(1)} %copy-done.5), kind=kOutput, calls=%fused_computation.1 | convolution fusion | flops 806354944 | bytes 5505024 | tf_op jit(solution)/shard_map/dot_general | solution.py:24
  78.0 5.0 %all-to-all-start.2 = ((bf16[4,256,512]{2,1,0:T(8,128)(2,1)}), bf16[4,256,512]{2,1,0:T(8,128)(2,1)S(1)}, u32[]{:S(2)}, u32[]{:S(2)}) async-start(bf16[4,256,512]{2,1,0:T(8,128)(2,1)} %add_convert_fusion), calls=%async_computation.2 | async-start | bytes 2097152 | tf_op jit(solution)/shard_map/all_to_all | solution.py:144
  83.0 2.5 %shard_map.65 = bf16[4,96,2048]{2,1,0:T(8,128)(2,1)} custom-call(s32[16]{0:T(128)S(1)} %stack.84.order_ref, bf16[96,8192]{1,0:T(8,128)(2,1)S(1)} %bitcast.85), custom_call_target="tpu_custom_call" | custom-call | bytes 3145728 | tf_op jit(solution)/shard_map/pallas_call | solution.py:53
  85.5 12.9 %all-to-all-done.2 = bf16[4,256,512]{2,1,0:T(8,128)(2,1)S(1)} async-done(((bf16[4,256,512]{2,1,0:T(8,128)(2,1)}), bf16[4,256,512]{2,1,0:T(8,128)(2,1)S(1)}, u32[]{:S(2)}, u32[]{:S(2)}) %all-to-all-start.2) | async-done | bytes 1048608 | tf_op jit(solution)/shard_map/all_to_all | solution.py:144
  98.6 5.9 %collective-permute-start.8 = (bf16[128,512]{1,0:T(8,128)(2,1)S(1)}, bf16[128,512]{1,0:T(8,128)(2,1)S(1)}, u32[]{:S(2)}, u32[]{:S(2)}) collective-permute-start(bf16[128,512]{1,0:T(8,128)(2,1)S(1)} %fusion.18), channel_id=1, source_target_pairs={{0,8},{2,10},{4,12},{6,14},{8,0},{10,2},{12,4},{14,6},{1,9},{3,11}... | collective-permute-start | bytes 393224 | tf_op jit(solution)/shard_map/ppermute | solution.py:32
  104.5 4.5 %collective-permute-start.9 = (bf16[128,512]{1,0:T(8,128)(2,1)S(1)}, bf16[128,512]{1,0:T(8,128)(2,1)S(1)}, u32[]{:S(2)}, u32[]{:S(2)}) collective-permute-start(bf16[128,512]{1,0:T(8,128)(2,1)S(1)} %fusion.18), channel_id=1, source_target_pairs={{0,4},{2,6},{4,0},{6,2},{8,12},{10,14},{12,8},{14,10},{1,5},{3,7},... | collective-permute-start | bytes 393224 | tf_op jit(solution)/shard_map/ppermute | solution.py:32
  109.0 2.0 %collective-permute-start.10 = (bf16[128,512]{1,0:T(8,128)(2,1)S(1)}, bf16[128,512]{1,0:T(8,128)(2,1)S(1)}, u32[]{:S(2)}, u32[]{:S(2)}) collective-permute-start(bf16[128,512]{1,0:T(8,128)(2,1)S(1)} %fusion.18), channel_id=1, source_target_pairs={{0,2},{2,0},{4,6},{6,4},{8,10},{10,8},{12,14},{14,12},{1,3},{3,1},... | collective-permute-start | bytes 393224 | tf_op jit(solution)/shard_map/ppermute | solution.py:32
  111.0 3.6 %all-to-all-start.3 = ((bf16[4,96,2048]{2,1,0:T(8,128)(2,1)}), bf16[4,96,2048]{2,1,0:T(8,128)(2,1)S(1)}, u32[]{:S(2)}, u32[]{:S(2)}) async-start(bf16[4,96,2048]{2,1,0:T(8,128)(2,1)} %shard_map.65), calls=%async_computation.3 | async-start | bytes 3145728 | tf_op jit(solution)/shard_map/all_to_all | solution.py:149
  114.6 3.5 %collective-permute-done.8 = bf16[128,512]{1,0:T(8,128)(2,1)S(1)} collective-permute-done((bf16[128,512]{1,0:T(8,128)(2,1)S(1)}, bf16[128,512]{1,0:T(8,128)(2,1)S(1)}, u32[]{:S(2)}, u32[]{:S(2)}) %collective-permute-start.8) | collective-permute-done | bytes 131104 | tf_op jit(solution)/shard_map/ppermute | solution.py:32
  122.9 6.0 %collective-permute-done.12 = bf16[128,512]{1,0:T(8,128)(2,1)S(1)} collective-permute-done((bf16[128,512]{1,0:T(8,128)(2,1)S(1)}, bf16[128,512]{1,0:T(8,128)(2,1)S(1)}, u32[]{:S(2)}, u32[]{:S(2)}) %collective-permute-start.12) | collective-permute-done | bytes 131104 | tf_op jit(solution)/shard_map/ppermute | solution.py:32
  128.9 4.7 %collective-permute-start.13 = (bf16[128,512]{1,0:T(8,128)(2,1)S(1)}, bf16[128,512]{1,0:T(8,128)(2,1)S(1)}, u32[]{:S(2)}, u32[]{:S(2)}) collective-permute-start(bf16[128,512]{1,0:T(8,128)(2,1)S(1)} %collective-permute-done.12), channel_id=1, source_target_pairs={{0,2},{2,0},{4,6},{6,4},{8,10},{10,8},{12,14},{14,12},{1,3},{3,1},... | collective-permute-start | bytes 393224 | tf_op jit(solution)/shard_map/ppermute | solution.py:32
  133.6 2.9 %collective-permute-done.13 = bf16[128,512]{1,0:T(8,128)(2,1)S(1)} collective-permute-done((bf16[128,512]{1,0:T(8,128)(2,1)S(1)}, bf16[128,512]{1,0:T(8,128)(2,1)S(1)}, u32[]{:S(2)}, u32[]{:S(2)}) %collective-permute-start.13) | collective-permute-done | bytes 131104 | tf_op jit(solution)/shard_map/ppermute | solution.py:32
  138.5 2.7 %collective-permute-done.14 = bf16[1024,512]{1,0:T(8,128)(2,1)} collective-permute-done((bf16[1024,512]{1,0:T(8,128)(2,1)S(1)}, bf16[1024,512]{1,0:T(8,128)(2,1)}, u32[]{:S(2)}, u32[]{:S(2)}) %collective-permute-start.14) | collective-permute-done | bytes 1048608 | tf_op jit(solution)/shard_map/ppermute | solution.py:33
  144.4 5.8 %all-to-all-start.4 = ((bf16[16,96,128]{2,1,0:T(8,128)(2,1)}), bf16[16,96,128]{2,1,0:T(8,128)(2,1)S(1)}, u32[]{:S(2)}, u32[]{:S(2)}) async-start(bf16[16,96,128]{2,1,0:T(8,128)(2,1)} %bitcast.41), calls=%async_computation.4 | async-start | bytes 786432 | tf_op jit(solution)/shard_map/all_to_all | solution.py:153
  150.3 10.4 %all-to-all-done.4 = bf16[16,96,128]{2,1,0:T(8,128)(2,1)S(1)} async-done(((bf16[16,96,128]{2,1,0:T(8,128)(2,1)}), bf16[16,96,128]{2,1,0:T(8,128)(2,1)S(1)}, u32[]{:S(2)}, u32[]{:S(2)}) %all-to-all-start.4) | async-done | bytes 393248 | tf_op jit(solution)/shard_map/all_to_all | solution.py:153
  161.2 10.7 %collective-permute-start.15 = (bf16[96,256]{0,1:T(8,128)(2,1)S(1)}, bf16[96,256]{0,1:T(8,128)(2,1)S(1)}, u32[]{:S(2)}, u32[]{:S(2)}) collective-permute-start(bf16[96,256]{0,1:T(8,128)(2,1)S(1)} %bitcast.91), channel_id=1, source_target_pairs={{0,256},{256,0},{1,257},{257,1},{2,258},{258,2},{3,259},{259,3},{4... | collective-permute-start | bytes 147464 | tf_op jit(solution)/shard_map/ppermute | solution.py:156
  172.1 6.8 %collective-permute-done.15 = bf16[96,256]{0,1:T(8,128)(2,1)S(1)} collective-permute-done((bf16[96,256]{0,1:T(8,128)(2,1)S(1)}, bf16[96,256]{0,1:T(8,128)(2,1)S(1)}, u32[]{:S(2)}, u32[]{:S(2)}) %collective-permute-start.15) | collective-permute-done | bytes 49184 | tf_op jit(solution)/shard_map/ppermute | solution.py:156
  (73 shorter events, 21.5 us)
Async XLA Ops:
  0.0 1.7 copy-start
  1.9 18.0 %collective-permute-start = (bf16[96,256]{1,0:T(8,128)(2,1)S(1)}, bf16[96,256]{1,0:T(8,128)(2,1)S(1)}, u32[]{:S(2)}, u32[]{:S(2)}) collective-permute-start(bf16[96,256]{1,0:T(8,128)(2,1)S(1)} %fusion.10), channel_id=1, source_target_pairs={{0,256},{256,0},{1,257},{257,1},{2,258},{258,2},{3,259},{259,3},{4... | collective-permute-start | bytes 147464 | tf_op jit(solution)/shard_map/ppermute | solution.py:134
  20.8 11.4 %all-to-all-start.1 = ((bf16[4,96,128]{2,1,0:T(8,128)(2,1)}), bf16[4,96,128]{2,1,0:T(8,128)(2,1)S(1)}, u32[]{:S(2)}, u32[]{:S(2)}) async-start(bf16[4,96,128]{2,1,0:T(8,128)(2,1)} %copy.16), calls=%async_computation.1 | async-start | bytes 196608 | tf_op jit(solution)/shard_map/all_to_all | solution.py:138
  25.4 1.4 copy-start.1
  26.8 1.4 copy-start.2
  32.2 41.6 %all-to-all-start = ((bf16[4,1536,256]{1,2,0:T(8,128)(2,1)}), bf16[4,1536,256]{1,2,0:T(8,128)(2,1)S(1)}, u32[]{:S(2)}, u32[]{:S(2)}) async-start(bf16[4,1536,256]{1,2,0:T(8,128)(2,1)} %copy.13), calls=%async_computation | async-start | bytes 6291456 | tf_op jit(solution)/shard_map/all_to_all | solution.py:140
  36.5 14.9 %collective-permute-start.1 = (bf16[96,512]{1,0:T(8,128)(2,1)S(1)}, bf16[96,512]{1,0:T(8,128)(2,1)S(1)}, u32[]{:S(2)}, u32[]{:S(2)}) collective-permute-start(bf16[96,512]{1,0:T(8,128)(2,1)S(1)} %copy_bitcast_fusion.1), channel_id=1, source_target_pairs={{0,8},{2,10},{4,12},{6,14},{8,0},{10,2},{12,4},{14,6},{1,9},{3,11}... | collective-permute-start | bytes 294920 | tf_op jit(solution)/shard_map/ppermute | solution.py:32
  42.4 9.5 %collective-permute-start.2 = (bf16[96,512]{1,0:T(8,128)(2,1)S(1)}, bf16[96,512]{1,0:T(8,128)(2,1)S(1)}, u32[]{:S(2)}, u32[]{:S(2)}) collective-permute-start(bf16[96,512]{1,0:T(8,128)(2,1)S(1)} %copy_bitcast_fusion.1), channel_id=1, source_target_pairs={{0,4},{2,6},{4,0},{6,2},{8,12},{10,14},{12,8},{14,10},{1,5},{3,7},... | collective-permute-start | bytes 294920 | tf_op jit(solution)/shard_map/ppermute | solution.py:32
  47.6 12.4 %collective-permute-start.3 = (bf16[96,512]{1,0:T(8,128)(2,1)S(1)}, bf16[96,512]{1,0:T(8,128)(2,1)S(1)}, u32[]{:S(2)}, u32[]{:S(2)}) collective-permute-start(bf16[96,512]{1,0:T(8,128)(2,1)S(1)} %copy_bitcast_fusion.1), channel_id=1, source_target_pairs={{0,2},{2,0},{4,6},{6,4},{8,10},{10,8},{12,14},{14,12},{1,3},{3,1},... | collective-permute-start | bytes 294920 | tf_op jit(solution)/shard_map/ppermute | solution.py:32
  51.9 13.3 %collective-permute-start.4 = (bf16[192,512]{1,0:T(8,128)(2,1)S(1)}, bf16[192,512]{1,0:T(8,128)(2,1)S(1)}, u32[]{:S(2)}, u32[]{:S(2)}) collective-permute-start(bf16[192,512]{1,0:T(8,128)(2,1)S(1)} %pad_maximum_fusion.1), channel_id=1, source_target_pairs={{0,2},{2,0},{4,6},{6,4},{8,10},{10,8},{12,14},{14,12},{1,3},{3,1},... | collective-permute-start | bytes 589832 | tf_op jit(solution)/shard_map/ppermute | solution.py:32
  55.5 7.4 %collective-permute-start.5 = (bf16[96,512]{1,0:T(8,128)(2,1)S(1)}, bf16[96,512]{1,0:T(8,128)(2,1)S(1)}, u32[]{:S(2)}, u32[]{:S(2)}) collective-permute-start(bf16[96,512]{1,0:T(8,128)(2,1)S(1)} %collective-permute-done.1), channel_id=1, source_target_pairs={{0,4},{2,6},{4,0},{6,2},{8,12},{10,14},{12,8},{14,10},{1,5},{3,7},... | collective-permute-start | bytes 294920 | tf_op jit(solution)/shard_map/ppermute | solution.py:32
  63.0 6.5 %collective-permute-start.6 = (bf16[96,512]{1,0:T(8,128)(2,1)S(1)}, bf16[96,512]{1,0:T(8,128)(2,1)S(1)}, u32[]{:S(2)}, u32[]{:S(2)}) collective-permute-start(bf16[96,512]{1,0:T(8,128)(2,1)S(1)} %collective-permute-done.5), channel_id=1, source_target_pairs={{0,2},{2,0},{4,6},{6,4},{8,10},{10,8},{12,14},{14,12},{1,3},{3,1},... | collective-permute-start | bytes 294920 | tf_op jit(solution)/shard_map/ppermute | solution.py:32
  69.5 1.9 %copy-start.4 = (bf16[768,512]{1,0:T(8,128)(2,1)}, bf16[768,512]{1,0:T(8,128)(2,1)S(1)}, u32[]{:S(2)}) copy-start(bf16[768,512]{1,0:T(8,128)(2,1)S(1)} %constant_dynamic-update-slice_fusion) | copy-start | bytes 2359300
  69.5 4.3 %collective-permute-start.7 = (bf16[768,512]{1,0:T(8,128)(2,1)S(1)}, bf16[768,512]{1,0:T(8,128)(2,1)}, u32[]{:S(2)}, u32[]{:S(2)}) collective-permute-start(bf16[768,512]{1,0:T(8,128)(2,1)S(1)} %constant_dynamic-update-slice_fusion), channel_id=1, source_target_pairs={{0,1},{1,0},{2,3},{3,2},{4,5},{5,4},{6,7},{7,6},{8,9},{9,8},{10,11... | collective-permute-start | bytes 2359304 | tf_op jit(solution)/shard_map/ppermute | solution.py:33
  73.8 2.2 %copy-start.5 = (bf16[768,512]{1,0:T(8,128)(2,1)S(1)}, bf16[768,512]{1,0:T(8,128)(2,1)}, u32[]{:S(2)}) copy-start(bf16[768,512]{1,0:T(8,128)(2,1)} %copy-done.4) | copy-start | bytes 2359300
  78.0 5.0 %copy-start.3 = (bf16[1,8192,96]{1,2,0:T(8,128)(2,1)S(1)}, bf16[1,8192,96]{1,2,0:T(8,128)(2,1)}, u32[]{:S(2)}) copy-start(bf16[1,8192,96]{1,2,0:T(8,128)(2,1)} %param.11) | copy-start | bytes 4718596
  78.0 20.4 %all-to-all-start.2 = ((bf16[4,256,512]{2,1,0:T(8,128)(2,1)}), bf16[4,256,512]{2,1,0:T(8,128)(2,1)S(1)}, u32[]{:S(2)}, u32[]{:S(2)}) async-start(bf16[4,256,512]{2,1,0:T(8,128)(2,1)} %add_convert_fusion), calls=%async_computation.2 | async-start | bytes 2097152 | tf_op jit(solution)/shard_map/all_to_all | solution.py:144
  98.6 19.5 %collective-permute-start.8 = (bf16[128,512]{1,0:T(8,128)(2,1)S(1)}, bf16[128,512]{1,0:T(8,128)(2,1)S(1)}, u32[]{:S(2)}, u32[]{:S(2)}) collective-permute-start(bf16[128,512]{1,0:T(8,128)(2,1)S(1)} %fusion.18), channel_id=1, source_target_pairs={{0,8},{2,10},{4,12},{6,14},{8,0},{10,2},{12,4},{14,6},{1,9},{3,11}... | collective-permute-start | bytes 393224 | tf_op jit(solution)/shard_map/ppermute | solution.py:32
  104.5 14.5 %collective-permute-start.9 = (bf16[128,512]{1,0:T(8,128)(2,1)S(1)}, bf16[128,512]{1,0:T(8,128)(2,1)S(1)}, u32[]{:S(2)}, u32[]{:S(2)}) collective-permute-start(bf16[128,512]{1,0:T(8,128)(2,1)S(1)} %fusion.18), channel_id=1, source_target_pairs={{0,4},{2,6},{4,0},{6,2},{8,12},{10,14},{12,8},{14,10},{1,5},{3,7},... | collective-permute-start | bytes 393224 | tf_op jit(solution)/shard_map/ppermute | solution.py:32
  109.0 13.9 %collective-permute-start.10 = (bf16[128,512]{1,0:T(8,128)(2,1)S(1)}, bf16[128,512]{1,0:T(8,128)(2,1)S(1)}, u32[]{:S(2)}, u32[]{:S(2)}) collective-permute-start(bf16[128,512]{1,0:T(8,128)(2,1)S(1)} %fusion.18), channel_id=1, source_target_pairs={{0,2},{2,0},{4,6},{6,4},{8,10},{10,8},{12,14},{14,12},{1,3},{3,1},... | collective-permute-start | bytes 393224 | tf_op jit(solution)/shard_map/ppermute | solution.py:32
  111.0 27.5 %all-to-all-start.3 = ((bf16[4,96,2048]{2,1,0:T(8,128)(2,1)}), bf16[4,96,2048]{2,1,0:T(8,128)(2,1)S(1)}, u32[]{:S(2)}, u32[]{:S(2)}) async-start(bf16[4,96,2048]{2,1,0:T(8,128)(2,1)} %shard_map.65), calls=%async_computation.3 | async-start | bytes 3145728 | tf_op jit(solution)/shard_map/all_to_all | solution.py:149
  119.0 14.6 %collective-permute-start.11 = (bf16[256,512]{1,0:T(8,128)(2,1)S(1)}, bf16[256,512]{1,0:T(8,128)(2,1)S(1)}, u32[]{:S(2)}, u32[]{:S(2)}) collective-permute-start(bf16[256,512]{1,0:T(8,128)(2,1)S(1)} %pad_maximum_fusion), channel_id=1, source_target_pairs={{0,2},{2,0},{4,6},{6,4},{8,10},{10,8},{12,14},{14,12},{1,3},{3,1},... | collective-permute-start | bytes 786440 | tf_op jit(solution)/shard_map/ppermute | solution.py:32
  120.9 8.0 %collective-permute-start.12 = (bf16[128,512]{1,0:T(8,128)(2,1)S(1)}, bf16[128,512]{1,0:T(8,128)(2,1)S(1)}, u32[]{:S(2)}, u32[]{:S(2)}) collective-permute-start(bf16[128,512]{1,0:T(8,128)(2,1)S(1)} %collective-permute-done.8), channel_id=1, source_target_pairs={{0,4},{2,6},{4,0},{6,2},{8,12},{10,14},{12,8},{14,10},{1,5},{3,7},... | collective-permute-start | bytes 393224 | tf_op jit(solution)/shard_map/ppermute | solution.py:32
  128.9 7.6 %collective-permute-start.13 = (bf16[128,512]{1,0:T(8,128)(2,1)S(1)}, bf16[128,512]{1,0:T(8,128)(2,1)S(1)}, u32[]{:S(2)}, u32[]{:S(2)}) collective-permute-start(bf16[128,512]{1,0:T(8,128)(2,1)S(1)} %collective-permute-done.12), channel_id=1, source_target_pairs={{0,2},{2,0},{4,6},{6,4},{8,10},{10,8},{12,14},{14,12},{1,3},{3,1},... | collective-permute-start | bytes 393224 | tf_op jit(solution)/shard_map/ppermute | solution.py:32
  136.5 4.7 %collective-permute-start.14 = (bf16[1024,512]{1,0:T(8,128)(2,1)S(1)}, bf16[1024,512]{1,0:T(8,128)(2,1)}, u32[]{:S(2)}, u32[]{:S(2)}) collective-permute-start(bf16[1024,512]{1,0:T(8,128)(2,1)S(1)} %constant_dynamic-update-slice_fusion.7), channel_id=1, source_target_pairs={{0,1},{1,0},{2,3},{3,2},{4,5},{5,4},{6,7},{7,6},{8,9},{9,8},{10,11... | collective-permute-start | bytes 3145736 | tf_op jit(solution)/shard_map/ppermute | solution.py:33
  143.0 7.2 %copy-start.6 = (f32[256,2]{0,1:T(2,128)S(1)}, f32[256,2]{0,1:T(2,128)}, u32[]{:S(2)}) copy-start(f32[256,2]{0,1:T(2,128)} %param.8) | copy-start | bytes 6148
  144.4 16.2 %all-to-all-start.4 = ((bf16[16,96,128]{2,1,0:T(8,128)(2,1)}), bf16[16,96,128]{2,1,0:T(8,128)(2,1)S(1)}, u32[]{:S(2)}, u32[]{:S(2)}) async-start(bf16[16,96,128]{2,1,0:T(8,128)(2,1)} %bitcast.41), calls=%async_computation.4 | async-start | bytes 786432 | tf_op jit(solution)/shard_map/all_to_all | solution.py:153
  161.2 17.7 %collective-permute-start.15 = (bf16[96,256]{0,1:T(8,128)(2,1)S(1)}, bf16[96,256]{0,1:T(8,128)(2,1)S(1)}, u32[]{:S(2)}, u32[]{:S(2)}) collective-permute-start(bf16[96,256]{0,1:T(8,128)(2,1)S(1)} %bitcast.91), channel_id=1, source_target_pairs={{0,256},{256,0},{1,257},{257,1},{2,258},{258,2},{3,259},{259,3},{4... | collective-permute-start | bytes 147464 | tf_op jit(solution)/shard_map/ppermute | solution.py:156
